TPU v7x, 128 devices: a whole 4x4x4 slice. The times are simulated.
128 devices in a mesh: pair: 8 (over y, core), virt: 16 (over x, z).
Axes of the slice: x: 4, y: 4, z: 4, core: 2. Of those that a mesh axis runs over, the one named last changes fastest.
Arguments:
- amplitudes: bfloat16 [2048, 16384], P(('pair', 'virt')), may hold values from -6 to 6
- tile_irreps: int32 [128], replicated, may hold values from 0 to 3, as said below
- ladder_blocks: bfloat16 [16384, 6144], P('virt'), as said below
Outputs:
- ladder_residual: bfloat16 [2048, 16384], P(('pair', 'virt'))
Inputs may be any that keep to these rules, and one draw needn't show every extreme that they name: `tile_irreps`: Non-decreasing along the tiles; each irrep holds at most 48 tiles and one holds exactly 48. Symmetric within an irrep: for pairs u and v of the same irrep g with u - first_g * 128 = j and v - first_g * 128 = k, ladder_blocks[u, k] == ladder_blocks[v, j]. Columns at or beyond count_g * 128 for rows of irrep g are not part of the operator.
All inputs are finite; a program needn't handle non-finite values.
Results may differ from a plain program's by a relative error of at most 0.0051.
Values may be sent and summed in bfloat16 or wider, within the bound.
No kernel may reach another device: no remote copies, remote signals or barrier semaphores. Data moves between devices by JAX's collectives and lax.ppermute only.
A program may use at most 192 MiB of HBM per device.

v0:
```python
import jax
import jax.numpy as jnp
from jax import lax
from jax.sharding import PartitionSpec as P

TILE = 128


def partner_2(block, axis, apart):
    count = lax.axis_size(axis)
    route = []
    for low in range(count):
        high = low | 1 << apart
        if high != low and high < count:
            route += [(low, high), (high, low)]
    return lax.ppermute(block, axis, route)


def sector_table(tile_irreps):
    irreps = jnp.arange(4, dtype=jnp.int32)
    lengths = jnp.sum((tile_irreps[None, :] == irreps[:, None]).astype(jnp.int32), axis=1)
    starts = jnp.cumsum(lengths) - lengths
    return (starts, lengths)


def ladder_rows(chosen, tile_irreps, ladder_blocks):
    width = chosen.shape[1]
    window = ladder_blocks.shape[1]
    owned = ladder_blocks.shape[0] // TILE
    virt_index = lax.axis_index("virt")
    starts, lengths = sector_table(tile_irreps)
    offsets = jnp.arange(window, dtype=jnp.int32)
    exchanged = lax.all_to_all(chosen, "virt", split_axis=1, concat_axis=0, tiled=True)
    total = jnp.zeros((chosen.shape[0] * lax.axis_size("virt"), width + window), jnp.float32)
    for local_tile in range(owned):
        irrep = tile_irreps[virt_index * owned + local_tile]
        contrib = jnp.dot(
            exchanged[:, local_tile * TILE : (local_tile + 1) * TILE],
            ladder_blocks[local_tile * TILE : (local_tile + 1) * TILE],
            preferred_element_type=jnp.float32,
        )
        contrib = jnp.where(
            offsets[None, :] < lengths[irrep] * TILE, contrib, jnp.zeros_like(contrib)
        )
        place = starts[irrep] * TILE
        current = lax.dynamic_slice_in_dim(total, place, window, 1)
        total = lax.dynamic_update_slice_in_dim(total, current + contrib, place, 1)
    summed = lax.psum_scatter(total[:, :width], "virt", scatter_dimension=0, tiled=True)
    return summed.astype(jnp.bfloat16)


def on_device(amplitudes, tile_irreps, ladder_blocks):
    top_bit = lax.axis_size("pair").bit_length() - 2
    partner = partner_2(amplitudes, "pair", top_bit)
    tau = (0.5 * (amplitudes.astype(jnp.float32) - partner.astype(jnp.float32))).astype(
        jnp.bfloat16
    )
    return ladder_rows(tau, tile_irreps, ladder_blocks)


def solution(mesh):
    placed = (P(("pair", "virt"), None), P(), P("virt", None))
    return jax.shard_map(
        on_device, mesh=mesh, in_specs=placed, out_specs=P(("pair", "virt"), None), check_vma=False
    )
```

profile of v0, /device:TPU:0, one launch (start us, length us, event | category | flops | bytes accessed | tf_op | source)
XLA Modules:
  0.0 240.8 jit_solution(4725484160299267505)
XLA Ops:
  6.5 3.3 %collective-permute-start = (bf16[16,16384]{1,0:T(8,128)(2,1)}, bf16[16,16384]{1,0:T(8,128)(2,1)S(1)}, u32[]{:S(2)}, u32[]{:S(2)}) collective-permute-start(bf16[16,16384]{1,0:T(8,128)(2,1)} %param.3), channel_id=1, source_target_pairs={{0,64},{64,0},{16,80},{80,16},{32,96},{96,32},{48,112},{112,48},{1... | collective-permute-start | bytes 1572872 | tf_op jit(solution)/shard_map/ppermute | solution.py:16
  9.8 1.6 fusion.33
  21.5 0.8 convert_reduce_fusion
  22.3 0.2 reduce-window.9
  27.5 0.7 fusion.31
  30.8 0.0 collective-permute-done
  30.8 1.2 multiply_convert_fusion
  32.1 0.8 copy.9
  32.9 7.9 %all-to-all-start = ((bf16[16,16,1024]{2,0,1:T(8,128)(2,1)}), bf16[16,16,1024]{2,0,1:T(8,128)(2,1)S(1)}, u32[]{:S(2)}, u32[]{:S(2)}) async-start(bf16[16,16,1024]{2,0,1:T(8,128)(2,1)} %bitcast.33), calls=%async_computation | async-start | bytes 1048576 | tf_op jit(solution)/shard_map/all_to_all | solution.py:33
  40.8 0.0 reduce-scatter.2.cloned.1.call-start
  48.4 3.6 %all-to-all-done = bf16[16,16,1024]{2,0,1:T(8,128)(2,1)S(1)} async-done(((bf16[16,16,1024]{2,0,1:T(8,128)(2,1)}), bf16[16,16,1024]{2,0,1:T(8,128)(2,1)S(1)}, u32[]{:S(2)}, u32[]{:S(2)}) %all-to-all-start) | async-done | bytes 524320 | tf_op jit(solution)/shard_map/all_to_all | solution.py:33
  52.0 0.0 slice-start
  52.0 0.0 slice-start.1
  52.0 10.3 %broadcast_in_dim.56 = f32[256,22528]{1,0:T(8,128)} broadcast(f32[]{:T(128)} %constant.43.clone.1), dimensions={} | broadcast | bytes 23068676 | tf_op jit(solution)/shard_map/broadcast_in_dim | solution.py:34
  62.3 0.0 slice-start.2
  62.3 5.2 %fusion = f32[256,22528]{1,0:T(8,128)} fusion(f32[256,22528]{1,0:T(8,128)} %broadcast_in_dim.56, s32[]{:T(128)S(6)} %select_n.115, pred[6144]{0:T(1024)(128)(4,1)S(1)} %iota_compare_fusion.7, bf16[1024,6144]{1,0:T(8,128)(2,1)} %param.5, bf16[256,1024]{1,0:T(8,128)(2,1)S(1)} %bitcast.36), kind=kOutput, calls=%fused_computation.8 | convolution fusion | flops 404226048 | bytes 7936004 | tf_op jit(solution)/shard_map/dot_general | solution.py:37
  67.6 6.9 %fusion.2 = f32[256,22528]{1,0:T(8,128)} fusion(f32[256,22528]{1,0:T(8,128)} %fusion, s32[]{:T(128)S(6)} %select_n.118, pred[6144]{0:T(1024)(128)(4,1)S(1)} %iota_compare_fusion.6, bf16[1024,6144]{1,0:T(8,128)(2,1)} %param.5, bf16[256,1024]{1,0:T(8,128)(2,1)S(1)} %bitcast.37), kind=kOutput, calls=%fused_computation.10 | convolution fusion | flops 405798912 | bytes 14227460 | tf_op jit(solution)/shard_map/dot_general | solution.py:37
  74.5 0.0 slice-done
  74.5 0.0 slice-done.1
  74.5 0.0 slice-done.2
  74.5 6.5 %fusion.4 = f32[256,22528]{1,0:T(8,128)} fusion(f32[256,22528]{1,0:T(8,128)} %fusion.2, s32[]{:T(128)S(6)} %select_n.122, pred[6144]{0:T(1024)(128)(4,1)S(1)} %iota_compare_fusion.5, bf16[1024,6144]{1,0:T(8,128)(2,1)S(1)} %bitcast.35, bf16[256,1024]{1,0:T(8,128)(2,1)S(1)} %bitcast.38), kind=kOutput, calls=%fused_computation.12 | convolution fusion | flops 405798912 | bytes 14227460 | tf_op jit(solution)/shard_map/dot_general | solution.py:37
  81.0 6.5 %fusion.6 = f32[256,22528]{1,0:T(8,128)} fusion(f32[256,22528]{1,0:T(8,128)} %fusion.4, s32[]{:T(128)S(6)} %select_n.126, pred[6144]{0:T(1024)(128)(4,1)S(1)} %iota_compare_fusion.4, bf16[1024,6144]{1,0:T(8,128)(2,1)S(1)} %bitcast.35, bf16[256,1024]{1,0:T(8,128)(2,1)S(1)} %bitcast.39), kind=kOutput, calls=%fused_computation.14 | convolution fusion | flops 405798912 | bytes 14227460 | tf_op jit(solution)/shard_map/dot_general | solution.py:37
  87.5 6.5 %fusion.8 = f32[256,22528]{1,0:T(8,128)} fusion(f32[256,22528]{1,0:T(8,128)} %fusion.6, s32[]{:T(128)S(6)} %select_n.130, pred[6144]{0:T(1024)(128)(4,1)S(1)} %iota_compare_fusion.3, bf16[1024,6144]{1,0:T(8,128)(2,1)S(1)} %bitcast.35, bf16[256,1024]{1,0:T(8,128)(2,1)S(1)} %bitcast.40), kind=kOutput, calls=%fused_computation.16 | convolution fusion | flops 405798912 | bytes 14227460 | tf_op jit(solution)/shard_map/dot_general | solution.py:37
  94.0 6.5 %fusion.10 = f32[256,22528]{1,0:T(8,128)} fusion(f32[256,22528]{1,0:T(8,128)} %fusion.8, s32[]{:T(128)S(6)} %select_n.134, pred[6144]{0:T(1024)(128)(4,1)S(1)} %iota_compare_fusion.2, bf16[1024,6144]{1,0:T(8,128)(2,1)S(1)} %bitcast.35, bf16[256,1024]{1,0:T(8,128)(2,1)S(1)} %bitcast.41), kind=kOutput, calls=%fused_computation.18 | convolution fusion | flops 405798912 | bytes 14227460 | tf_op jit(solution)/shard_map/dot_general | solution.py:37
  100.5 6.5 %fusion.12 = f32[256,22528]{1,0:T(8,128)} fusion(f32[256,22528]{1,0:T(8,128)} %fusion.10, s32[]{:T(128)S(6)} %select_n.138, pred[6144]{0:T(1024)(128)(4,1)S(1)} %iota_compare_fusion.1, bf16[1024,6144]{1,0:T(8,128)(2,1)S(1)} %bitcast.35, bf16[256,1024]{1,0:T(8,128)(2,1)S(1)} %bitcast.42), kind=kOutput, calls=%fused_computation.20 | convolution fusion | flops 405798912 | bytes 14227460 | tf_op jit(solution)/shard_map/dot_general | solution.py:37
  107.0 6.5 %fusion.14 = f32[256,22528]{1,0:T(8,128)} fusion(f32[256,22528]{1,0:T(8,128)} %fusion.12, s32[]{:T(128)S(6)} %select_n.142, pred[6144]{0:T(1024)(128)(4,1)S(1)} %iota_compare_fusion, bf16[1024,6144]{1,0:T(8,128)(2,1)S(1)} %bitcast.35, bf16[256,1024]{1,0:T(8,128)(2,1)S(1)} %bitcast.43), kind=kOutput, calls=%fused_computation.22 | convolution fusion | flops 405798912 | bytes 14227460 | tf_op jit(solution)/shard_map/dot_general | solution.py:37
  113.5 11.3 %slice.76 = f32[256,16384]{1,0:T(8,128)} slice(f32[256,22528]{1,0:T(8,128)} %fusion.14), slice={[0:256], [0:16384]} | slice | bytes 33554432 | tf_op jit(solution)/shard_map/slice | solution.py:48
  124.8 0.0 reduce-scatter.2.cloned.1.call-update
  124.9 107.0 %reduce-scatter.2.cloned.1.call-done = f32[16,16384]{1,0:T(8,128)} async-done(((f32[256,16384]{1,0:T(8,128)}), f32[16,16384]{1,0:T(8,128)}) %reduce-scatter.2.cloned.1.call-update) | async-done | bytes 1048592 | tf_op jit(solution)/shard_map/reduce_scatter | solution.py:48
  231.9 2.1 convert_element_type.19
  (10 shorter events, 0.1 us)
Async XLA Ops:
  6.5 24.3 %collective-permute-start = (bf16[16,16384]{1,0:T(8,128)(2,1)}, bf16[16,16384]{1,0:T(8,128)(2,1)S(1)}, u32[]{:S(2)}, u32[]{:S(2)}) collective-permute-start(bf16[16,16384]{1,0:T(8,128)(2,1)} %param.3), channel_id=1, source_target_pairs={{0,64},{64,0},{16,80},{80,16},{32,96},{96,32},{48,112},{112,48},{1... | collective-permute-start | bytes 1572872 | tf_op jit(solution)/shard_map/ppermute | solution.py:16
  32.9 19.1 %all-to-all-start = ((bf16[16,16,1024]{2,0,1:T(8,128)(2,1)}), bf16[16,16,1024]{2,0,1:T(8,128)(2,1)S(1)}, u32[]{:S(2)}, u32[]{:S(2)}) async-start(bf16[16,16,1024]{2,0,1:T(8,128)(2,1)} %bitcast.33), calls=%async_computation | async-start | bytes 1048576 | tf_op jit(solution)/shard_map/all_to_all | solution.py:33
  40.8 191.1 %reduce-scatter.2.cloned.1.call-start = ((), (), s32[]{:S(2)}) async-start(), calls=%async_computation.2 | async-start | bytes 17825792 | tf_op jit(solution)/shard_map/reduce_scatter | solution.py:48
  52.0 22.5 %slice-start = ((s8[12582912]{0:T(1024)(128)(4,1)}), s8[4194304]{0:T(1024)(128)(4,1)S(1)}, s32[]{:S(2)}) async-start(s8[12582912]{0:T(1024)(128)(4,1)} %bitcast.34), calls=%async_computation.3 | async-start | bytes 8388608
  52.0 22.5 %slice-start.1 = ((s8[12582912]{0:T(1024)(128)(4,1)}), s8[4194304]{0:T(1024)(128)(4,1)S(1)}, s32[]{:S(2)}) async-start(s8[12582912]{0:T(1024)(128)(4,1)} %bitcast.34), calls=%async_computation.4 | async-start | bytes 8388608
  62.3 12.2 %slice-start.2 = ((s8[12582912]{0:T(1024)(128)(4,1)}), s8[4194304]{0:T(1024)(128)(4,1)S(1)}, s32[]{:S(2)}) async-start(s8[12582912]{0:T(1024)(128)(4,1)} %bitcast.34), calls=%async_computation.5 | async-start | bytes 8388608
Sparse Core Ops, SparseCore 0:
  125.0 106.8 reduce-scatter.1
where the time goes:
time: 242 us; the launch traced here: 241 us
  waiting for transfers between devices  111 us (46%)
  matrix products  51.1 us (21%)
  between operations  38.6 us (16%)
  local copies, waits for them, and re-layouts  24.9 us (10%)
  starting transfers between devices  11.2 us (5%)
  other arithmetic  4.32 us (2%)
    reduce_scatter x1, waiting for transfers between devices, ladder_rows(): lax.psum_scatter(total[:, :width], 'virt', scatter_dimension=0, tiled=True)  107 us
    dot_general x8, matrix products, ladder_rows(): jnp.dot(exchanged[:, local_tile * TILE:(local_tile + 1) * TILE], ladder_b...  51.1 us
    slice x1, local copies, waits for them, and re-layouts, ladder_rows(): total[:, :width]  11.3 us
    broadcast_in_dim x1, local copies, waits for them, and re-layouts, ladder_rows(): jnp.zeros((chosen.shape[0] * lax.axis_size('virt'), width + window), jnp....  10.3 us
    all_to_all x1, starting transfers between devices, ladder_rows(): lax.all_to_all(chosen, 'virt', split_axis=1, concat_axis=0, tiled=True)  7.88 us
  transfers between devices with their start and end apart: 3, of which 2 were waited for; matrix products, arithmetic and copies ran while one was open for 1% of the time, Pallas kernels for 0%

commit v1 on v0

v1 whole, which is shorter than its diff:
```python
import functools

import jax
import jax.numpy as jnp
from jax import lax
from jax.experimental import pallas as pl
from jax.experimental.pallas import tpu as pltpu
from jax.sharding import Mesh, PartitionSpec as P

TILE = 128
IRREPS = 4
TILES = 128
SECT = 48
OWNED = 8
VIRT = 16
ROWS = 8
EXTRA = 5
SLOTS = SECT + EXTRA
SIDE = 4
OUT_SLOTS = OWNED + 2 * SIDE
MAIN = 8


def clip_count(first, count, w):
    low, high = jnp.maximum(first, w * OWNED), jnp.minimum(first + count, w * OWNED + OWNED)
    return jnp.maximum(high - low, 0)


def plan_kernel(irreps_ref, table_ref):
    def count(at, counts):
        irrep = irreps_ref[at]
        return tuple(counts[g] + (irrep == g).astype(jnp.int32) for g in range(IRREPS))

    counts = lax.fori_loop(0, TILES, count, (jnp.int32(0),) * IRREPS)
    first = jnp.int32(0)
    firsts = []
    for g in range(IRREPS):
        firsts.append(first)
        table_ref[g] = first
        table_ref[IRREPS + g] = counts[g]
        first = first + counts[g]
    for w in range(VIRT):
        best, main = clip_count(firsts[0], counts[0], w), jnp.int32(0)
        for g in range(1, IRREPS):
            held = clip_count(firsts[g], counts[g], w)
            main = jnp.where(held > best, g, main)
            best = jnp.maximum(held, best)
        table_ref[MAIN + w] = main


def plan(tile_irreps):
    return pl.pallas_call(
        plan_kernel,
        out_shape=jax.ShapeDtypeStruct((32,), jnp.int32),
        in_specs=[pl.BlockSpec(memory_space=pltpu.SMEM)],
        out_specs=pl.BlockSpec(memory_space=pltpu.SMEM),
        name="plan",
    )(tile_irreps)


def position(table_ref, w):
    main = table_ref[MAIN + w]
    first, count = table_ref[main], table_ref[IRREPS + main]
    before = jnp.maximum(first - w * OWNED, 0)
    return main, first, count, before, clip_count(first, count, w)


def pack_kernel(table_ref, place_ref, own_ref, partner_ref, out_ref, tau_ref):
    lower = place_ref[0] == 1
    for tile in range(TILES):
        columns = pl.ds(tile * TILE, TILE)
        own = own_ref[:, columns].astype(jnp.float32)
        mine = jnp.where(lower, own[ROWS:], own[:ROWS])
        other = partner_ref[:, columns].astype(jnp.float32)
        tau_ref[tile] = (0.5 * (mine - other)).astype(jnp.bfloat16)
    tau_ref[TILES] = jnp.zeros((ROWS, TILE), jnp.bfloat16)

    @pl.loop(0, VIRT)
    def _(w):
        _, first, count, before, held = position(table_ref, w)
        for slot in range(SECT):
            out_ref[w, slot] = tau_ref[jnp.where(slot < count, first + slot, TILES)]
        for extra in range(EXTRA):
            at = jnp.where(extra < before, extra, extra + held)
            at = jnp.where(at < OWNED, w * OWNED + at, TILES)
            out_ref[w, SECT + extra] = tau_ref[at]


def pack(table, place, own, partner):
    return pl.pallas_call(
        pack_kernel,
        out_shape=jax.ShapeDtypeStruct((VIRT, SLOTS, ROWS, TILE), jnp.bfloat16),
        in_specs=[pl.BlockSpec(memory_space=pltpu.SMEM)] * 2 + [pl.BlockSpec(memory_space=pltpu.VMEM)] * 2,
        out_specs=pl.BlockSpec(memory_space=pltpu.VMEM),
        scratch_shapes=[pltpu.VMEM((TILES + 1, ROWS, TILE), jnp.bfloat16)],
        compiler_params=pltpu.CompilerParams(vmem_limit_bytes=40 << 20),
        name="pack",
    )(table, place, own, partner)


GROUP = 2
NT = (((1,), (1,)), ((), ()))
NN = (((1,), (0,)), ((), ()))


def right_start(first, last_block):
    return jnp.minimum(last_block * OWNED - first, SECT - SIDE)


def ladder_kernel(
    table_ref, place_ref, irreps_ref, tau_ref, block_ref, out_ref, held_ref, left_ref, right_ref, own_ref, total_ref
):
    step = pl.program_id(0)
    w = place_ref[1]
    main, first, _, before, held = position(table_ref, w)

    @pl.when(step == 0)
    def _():
        for slot in range(SLOTS):
            for src in range(0, VIRT, 2):
                rows = jnp.concatenate([tau_ref[src, slot], tau_ref[src + 1, slot]], axis=0)
                held_ref[pl.ds(src * ROWS, 2 * ROWS), pl.ds(slot * TILE, TILE)] = rows
        left_ref[...] = jnp.zeros_like(left_ref)
        right_ref[...] = jnp.zeros_like(right_ref)

    def tau_of(tile):
        inside = w * OWNED + tile - first
        outside = SECT + jnp.where(tile < before, tile, tile - held)
        slot = jnp.where(irreps_ref[w * OWNED + tile] == main, inside, outside)
        return held_ref[:, pl.ds(pl.multiple_of(slot * TILE, TILE), TILE)]

    def send(slot, values):
        values = values.astype(jnp.bfloat16)
        for dest in range(VIRT):
            rows = values[dest * ROWS : (dest + 1) * ROWS]
            out_ref[dest, slot] = rows
            out_ref[VIRT + dest, slot] = rows

    total_ref[...] = lax.dot_general(
        held_ref[:, : SECT * TILE], block_ref[...], NT, preferred_element_type=jnp.float32
    )
    left_irrep = irreps_ref[w * OWNED]
    left_first = table_ref[left_irrep]
    left_block = left_first // OWNED
    left_on = (left_block != w) & (table_ref[MAIN + left_block] != left_irrep)
    right_irrep = irreps_ref[w * OWNED + OWNED - 1]
    right_first = table_ref[right_irrep]
    right_block = (right_first + table_ref[IRREPS + right_irrep] - 1) // OWNED
    right_on = (right_block != w) & (table_ref[MAIN + right_block] != right_irrep)
    for part in range(GROUP):
        tile = step * GROUP + part
        rows = pl.ds(part * TILE, TILE)
        irrep = irreps_ref[w * OWNED + tile]
        own_ref[...] = total_ref[:, part * TILE : (part + 1) * TILE]

        @pl.when(irrep != main)
        def _():
            own_ref[...] = jnp.zeros_like(own_ref)

            @pl.loop(0, OWNED)
            def _(other):
                @pl.when(irreps_ref[w * OWNED + other] == irrep)
                def _():
                    at = (w * OWNED + other - table_ref[irrep]) * TILE
                    own_ref[...] += lax.dot_general(
                        tau_of(other),
                        block_ref[rows, pl.ds(pl.multiple_of(at, TILE), TILE)],
                        NT,
                        preferred_element_type=jnp.float32,
                    )

        send(tile, own_ref[...])

        @pl.when(left_on & (irrep == left_irrep))
        def _():
            left_ref[...] += lax.dot_general(
                tau_of(tile), block_ref[rows, : SIDE * TILE], NN, preferred_element_type=jnp.float32
            )

        @pl.when(right_on & (irrep == right_irrep))
        def _():
            at = pl.multiple_of(right_start(right_first, right_block) * TILE, TILE)
            right_ref[...] += lax.dot_general(
                tau_of(tile), block_ref[rows, pl.ds(at, SIDE * TILE)], NN, preferred_element_type=jnp.float32
            )

    @pl.when(step == OWNED // GROUP - 1)
    def _():
        for side in range(SIDE):
            send(OWNED + side, left_ref[:, side * TILE : (side + 1) * TILE])
            send(OWNED + SIDE + side, right_ref[:, side * TILE : (side + 1) * TILE])


def ladder(table, place, tile_irreps, taken, blocks):
    rows = VIRT * ROWS
    window = SECT * TILE
    return pl.pallas_call(
        ladder_kernel,
        out_shape=jax.ShapeDtypeStruct((2 * VIRT, OUT_SLOTS, ROWS, TILE), jnp.bfloat16),
        grid_spec=pltpu.PrefetchScalarGridSpec(
            num_scalar_prefetch=3,
            grid=(OWNED // GROUP,),
            in_specs=[
                pl.BlockSpec((VIRT, SLOTS, ROWS, TILE), lambda i, *_: (0, 0, 0, 0)),
                pl.BlockSpec((GROUP * TILE, window), lambda i, *_: (i, 0)),
            ],
            out_specs=pl.BlockSpec((2 * VIRT, OUT_SLOTS, ROWS, TILE), lambda i, *_: (0, 0, 0, 0)),
            scratch_shapes=[
                pltpu.VMEM((rows, SLOTS * TILE), jnp.bfloat16),
                pltpu.VMEM((rows, SIDE * TILE), jnp.float32),
                pltpu.VMEM((rows, SIDE * TILE), jnp.float32),
                pltpu.VMEM((rows, TILE), jnp.float32),
                pltpu.VMEM((rows, GROUP * TILE), jnp.float32),
            ],
        ),
        compiler_params=pltpu.CompilerParams(vmem_limit_bytes=48 << 20),
        cost_estimate=pl.CostEstimate(
            flops=2 * rows * window * OWNED * TILE, bytes_accessed=16 << 20, transcendentals=0
        ),
        name="ladder",
    )(table, place, tile_irreps, taken, blocks)


def collect_kernel(table_ref, place_ref, irreps_ref, taken_ref, out_ref):
    lower = place_ref[0] == 1
    signs = (jnp.where(lower, -1.0, 1.0), jnp.where(lower, 1.0, -1.0))

    @pl.loop(0, VIRT)
    def _(w):
        for tile in range(OWNED):
            both = [taken_ref[half * VIRT + w, tile].astype(jnp.float32) * signs[half] for half in range(2)]
            columns = pl.ds(pl.multiple_of((w * OWNED + tile) * TILE, TILE), TILE)
            out_ref[:, columns] = jnp.concatenate(both, axis=0).astype(jnp.bfloat16)
        main, _, _, _, held = position(table_ref, w)

        @pl.when(held < OWNED)
        def _():
            @pl.loop(0, OWNED)
            def _(tile):
                at = w * OWNED + tile
                irrep = irreps_ref[at]

                @pl.when(irrep != main)
                def _():
                    first = table_ref[irrep]
                    left_block = first // OWNED
                    right_block = (first + table_ref[IRREPS + irrep] - 1) // OWNED
                    on_left = w == left_block
                    low = jnp.where(on_left, left_block + 1, left_block)
                    high = jnp.where(on_left, right_block + 1, right_block)
                    slot = jnp.where(
                        on_left,
                        OWNED + at - first,
                        OWNED + SIDE + at - first - right_start(first, right_block),
                    )
                    both = []
                    for half in range(2):
                        total = lax.fori_loop(
                            low,
                            high,
                            lambda v, total: total + taken_ref[half * VIRT + v, slot].astype(jnp.float32),
                            taken_ref[half * VIRT + w, tile].astype(jnp.float32),
                        )
                        both.append(total * signs[half])
                    columns = pl.ds(pl.multiple_of(at * TILE, TILE), TILE)
                    out_ref[:, columns] = jnp.concatenate(both, axis=0).astype(jnp.bfloat16)


def collect(table, place, tile_irreps, taken):
    return pl.pallas_call(
        collect_kernel,
        out_shape=jax.ShapeDtypeStruct((2 * ROWS, TILES * TILE), jnp.bfloat16),
        in_specs=[pl.BlockSpec(memory_space=pltpu.SMEM)] * 3 + [pl.BlockSpec(memory_space=pltpu.VMEM)],
        out_specs=pl.BlockSpec(memory_space=pltpu.VMEM),
        compiler_params=pltpu.CompilerParams(vmem_limit_bytes=40 << 20),
        name="collect",
    )(table, place, tile_irreps, taken)


def on_device(amplitudes, tile_irreps, ladder_blocks):
    half = lax.axis_index("half")
    place = jnp.stack([half, lax.axis_index("virt")]).astype(jnp.int32)
    sent = lax.dynamic_slice_in_dim(amplitudes, (1 - half) * ROWS, ROWS, 0)
    partner = lax.ppermute(sent, "half", [(0, 1), (1, 0)])
    table = plan(tile_irreps)
    packed = pack(table, place, amplitudes, partner)
    taken = lax.all_to_all(packed, "virt", split_axis=0, concat_axis=0, tiled=True)
    sums = ladder(table, place, tile_irreps, taken, ladder_blocks)
    taken = lax.all_to_all(sums, ("half", "virt"), split_axis=0, concat_axis=0, tiled=True)
    return collect(table, place, tile_irreps, taken)


def solution(mesh):
    pairs, virt = mesh.devices.shape
    split = Mesh(mesh.devices.reshape(2, pairs // 2, virt), ("half", "quarter", "virt"))
    rows = P(("half", "quarter", "virt"), None)
    return jax.shard_map(
        on_device, mesh=split, in_specs=(rows, P(), P("virt", None)), out_specs=rows, check_vma=False
    )
```

time: 242 us -> 80.6 us (0.33)
  waiting for transfers between devices: 111 us -> 3.23 us
  blocking collectives: 0 us -> 54.4 us
  matrix products: 51.1 us -> 0 us
  between operations: 38.6 us -> 0.05 us
  local copies, waits for them, and re-layouts: 24.9 us -> 2.68 us
  Pallas kernels: 0 us -> 16 us
  starting transfers between devices: 11.2 us -> 3.36 us
  other arithmetic: 4.32 us -> 0.08 us
    reduce_scatter x1 -> x0, waiting for transfers between devices: 107 us -> none  [ladder_rows(): lax.psum_scatter(total[:, :width], 'virt', scatter_dimension=0, tiled=True)]
    all_to_all x0 -> x2, blocking collectives: none -> 54.4 us  [the longest x1 31.1 us: on_device(): lax.all_to_all(packed, 'virt', split_axis=0, concat_axis=0, tiled=True)]
    dot_general x8 -> x0, matrix products: 51.1 us -> none  [ladder_rows(): jnp.dot(exchanged[:, local_tile * TILE:(local_tile + 1) * TILE], ladder_b...]
    pallas_call x0 -> x4, Pallas kernels: none -> 16 us  [the longest x1 8.68 us: ladder(): pl.pallas_call(ladder_kernel, out_shape=jax.ShapeDtypeStruct((2 * VIRT, O...]
    slice x1 -> x0, local copies, waits for them, and re-layouts: 11.3 us -> none  [ladder_rows(): total[:, :width]]
    broadcast_in_dim x1 -> x0, local copies, waits for them, and re-layouts: 10.3 us -> none  [ladder_rows(): jnp.zeros((chosen.shape[0] * lax.axis_size('virt'), width + window), jnp....]
    all_to_all x1 -> x0, starting transfers between devices: 7.88 us -> none  [ladder_rows(): lax.all_to_all(chosen, 'virt', split_axis=1, concat_axis=0, tiled=True)]
    all_to_all x1 -> x0, waiting for transfers between devices: 3.59 us -> none  [ladder_rows(): lax.all_to_all(chosen, 'virt', split_axis=1, concat_axis=0, tiled=True)]
  transfers between devices with their start and end apart: 3 -> 1, of which waited for: 2 -> 1; matrix products, arithmetic and copies ran while one was open for 1% -> 0% of each run, Pallas kernels for 0% -> 4%
where the time goes in v1:
time: 80.6 us; the launch traced here: 79.7 us
  blocking collectives  54.4 us (67%)
  Pallas kernels  16 us (20%)
  starting transfers between devices  3.36 us (4%)
  waiting for transfers between devices  3.23 us (4%)
  local copies, waits for them, and re-layouts  2.68 us (3%)
    all_to_all x1, blocking collectives, on_device(): lax.all_to_all(packed, 'virt', split_axis=0, concat_axis=0, tiled=True)  31.1 us
    all_to_all x1, blocking collectives, on_device(): lax.all_to_all(sums, ('half', 'virt'), split_axis=0, concat_axis=0, tiled...  23.2 us
    pallas_call x1, Pallas kernels, ladder(): pl.pallas_call(ladder_kernel, out_shape=jax.ShapeDtypeStruct((2 * VIRT, O...  8.68 us
    ppermute x1, starting transfers between devices, on_device(): partner = lax.ppermute(sent, 'half', [(0, 1), (1, 0)])  3.36 us
    ppermute x1, waiting for transfers between devices, on_device(): partner = lax.ppermute(sent, 'half', [(0, 1), (1, 0)])  3.23 us
    pallas_call x1, Pallas kernels, plan(): pl.pallas_call(plan_kernel, out_shape=jax.ShapeDtypeStruct((32,), jnp.int...  2.99 us
    pallas_call x1, Pallas kernels, collect(): pl.pallas_call(collect_kernel, out_shape=jax.ShapeDtypeStruct((2 * ROWS,...  2.25 us
    pallas_call x1, Pallas kernels, pack(): pl.pallas_call(pack_kernel, out_shape=jax.ShapeDtypeStruct((VIRT, SLOTS,...  2.05 us
  transfers between devices with their start and end apart: 1, of which 1 were waited for; matrix products, arithmetic and copies ran while one was open for 0% of the time, Pallas kernels for 4%

profile of v1, /device:TPU:0, one launch (start us, length us, event | category | flops | bytes accessed | tf_op | source)
XLA Modules:
  0.0 79.7 jit_solution(14286505124093188357)
XLA Ops:
  0.0 1.0 %constant_dynamic-slice_fusion = bf16[8,16384]{1,0:T(8,128)(2,1)S(1)} fusion(bf16[16,16384]{1,0:T(8,128)(2,1)} %own_ref.1, s32[]{:T(128)S(6)} %select_n.3), kind=kLoop, calls=%fused_computation.1 | loop fusion | bytes 524292 | tf_op jit(solution)/shard_map/dynamic_slice | solution.py:283
  1.0 3.4 %collective-permute-start = (bf16[8,16384]{1,0:T(8,128)(2,1)S(1)}, bf16[8,16384]{1,0:T(8,128)(2,1)S(1)}, u32[]{:S(2)}, u32[]{:S(2)}) collective-permute-start(bf16[8,16384]{1,0:T(8,128)(2,1)S(1)} %constant_dynamic-slice_fusion), channel_id=1, source_target_pairs={{0,64},{64,0},{1,65},{65,1},{2,66},{66,2},{3,67},{67,3},{4,68},{68... | collective-permute-start | bytes 786440 | tf_op jit(solution)/shard_map/ppermute | solution.py:284
  4.3 3.0 %plan.1.table_ref = s32[32]{0:T(128)} custom-call(s32[128]{0:T(128)} %irreps_ref.5), custom_call_target="tpu_custom_call" | custom-call | tf_op jit(solution)/shard_map/plan/pallas_call | solution.py:52
  7.3 0.1 pad_add_fusion.place_ref
  7.4 3.2 %collective-permute-done.partner_ref = bf16[8,16384]{1,0:T(8,128)(2,1)S(1)} collective-permute-done((bf16[8,16384]{1,0:T(8,128)(2,1)S(1)}, bf16[8,16384]{1,0:T(8,128)(2,1)S(1)}, u32[]{:S(2)}, u32[]{:S(2)}) %collective-permute-start) | collective-permute-done | bytes 262176 | tf_op jit(solution)/shard_map/ppermute | solution.py:284
  10.6 0.0 copy-start
  10.6 1.0 %copy-done = bf16[16,16384]{1,0:T(8,128)(2,1)S(1)} copy-done((bf16[16,16384]{1,0:T(8,128)(2,1)S(1)}, bf16[16,16384]{1,0:T(8,128)(2,1)}, u32[]{:S(2)}) %copy-start) | copy-done | bytes 524312
  11.7 0.0 copy-start.1
  11.7 0.7 copy-done.1
  12.3 2.1 %pack.1 = bf16[16,53,8,128]{3,2,1,0:T(8,128)(2,1)S(1)} custom-call(s32[32]{0:T(128)S(1)} %copy-done.1, s32[2]{0:T(128)S(1)} %pad_add_fusion.place_ref, bf16[16,16384]{1,0:T(8,128)(2,1)S(1)} %copy-done, bf16[8,16384]{1,0:T(8,128)(2,1)S(1)} %collective-permute-done.partner_ref), custom_call_target="tpu_custom_call" | custom-call | tf_op jit(solution)/shard_map/pack/pallas_call | solution.py:90
  14.4 0.0 copy-start.2
  14.4 0.0 copy-start.3
  14.4 31.1 %all_to_all.10.tau_ref = bf16[16,53,8,128]{3,2,1,0:T(8,128)(2,1)S(1)} all-to-all(bf16[16,53,8,128]{3,2,1,0:T(8,128)(2,1)S(1)} %pack.1), channel_id=1, replica_groups=mesh['half'=2,'quarter'=4,'virt'=16] {'virt'}, dimensions={0} | all-to-all | bytes 3473408 | tf_op jit(solution)/shard_map/all_to_all | solution.py:287
  45.6 0.0 copy-done.2
  45.6 0.0 copy-done.3
  45.6 8.7 %ladder.1 = bf16[32,16,8,128]{3,2,1,0:T(8,128)(2,1)S(1)} custom-call(s32[32]{0:T(128)S(1)} %copy-done.2, s32[2]{0:T(128)S(1)} %pad_add_fusion.place_ref, s32[128]{0:T(128)S(1)} %copy-done.3, bf16[16,53,8,128]{3,2,1,0:T(8,128)(2,1)S(1)} %all_to_all.10.tau_ref, bf16[1024,6144]{1,0:T(8,128)(2,1)} %block_ref.1), custom_call_target="tpu_custom_call" | custom-call | flops 1610612736 | bytes 16777216 | tf_op jit(solution)/shard_map/ladder/pallas_call | solution.py:197
  54.3 23.2 %all_to_all.11.taken_ref = bf16[32,16,8,128]{3,2,1,0:T(8,128)(2,1)S(1)} all-to-all(bf16[32,16,8,128]{3,2,1,0:T(8,128)(2,1)S(1)} %ladder.1), channel_id=1, replica_groups=mesh['half'=2,'quarter'=4,'virt'=16] {'half','virt'}, dimensions={0} | all-to-all | bytes 2097152 | tf_op jit(solution)/shard_map/all_to_all | solution.py:289
  77.5 2.3 %collect.1 = bf16[16,16384]{1,0:T(8,128)(2,1)} custom-call(s32[32]{0:T(128)S(1)} %copy-done.2, s32[2]{0:T(128)S(1)} %pad_add_fusion.place_ref, s32[128]{0:T(128)S(1)} %copy-done.3, bf16[32,16,8,128]{3,2,1,0:T(8,128)(2,1)S(1)} %all_to_all.11.taken_ref), custom_call_target="tpu_custom_call" | custom-call | tf_op jit(solution)/shard_map/collect/pallas_call | solution.py:270
Async XLA Ops:
  1.0 9.7 %collective-permute-start = (bf16[8,16384]{1,0:T(8,128)(2,1)S(1)}, bf16[8,16384]{1,0:T(8,128)(2,1)S(1)}, u32[]{:S(2)}, u32[]{:S(2)}) collective-permute-start(bf16[8,16384]{1,0:T(8,128)(2,1)S(1)} %constant_dynamic-slice_fusion), channel_id=1, source_target_pairs={{0,64},{64,0},{1,65},{65,1},{2,66},{66,2},{3,67},{67,3},{4,68},{68... | collective-permute-start | bytes 786440 | tf_op jit(solution)/shard_map/ppermute | solution.py:284
  10.6 1.0 %copy-start = (bf16[16,16384]{1,0:T(8,128)(2,1)S(1)}, bf16[16,16384]{1,0:T(8,128)(2,1)}, u32[]{:S(2)}) copy-start(bf16[16,16384]{1,0:T(8,128)(2,1)} %own_ref.1) | copy-start | bytes 1572868
  11.7 0.7 copy-start.1
  14.4 31.2 %copy-start.2 = (s32[32]{0:T(128)S(1)}, s32[32]{0:T(128)}, u32[]{:S(2)}) copy-start(s32[32]{0:T(128)} %plan.1.table_ref) | copy-start | bytes 388
  14.4 31.2 %copy-start.3 = (s32[128]{0:T(128)S(1)}, s32[128]{0:T(128)}, u32[]{:S(2)}) copy-start(s32[128]{0:T(128)} %irreps_ref.5) | copy-start | bytes 1540

commit v2 on v1

v2 whole, which is shorter than its diff:
```python
import functools

import jax
import jax.numpy as jnp
from jax import lax
from jax.experimental import pallas as pl
from jax.experimental.pallas import tpu as pltpu
from jax.sharding import Mesh, PartitionSpec as P

TILE = 128
IRREPS = 4
TILES = 128
SECT = 48
OWNED = 8
VIRT = 16
ROWS = 8
EXTRA = 5
SLOTS = SECT + EXTRA
SIDE = 4
OUT_SLOTS = OWNED + 2 * SIDE
MAIN = 8
HALF, PLACE = 32, 33


def clip_count(first, count, w):
    low, high = jnp.maximum(first, w * OWNED), jnp.minimum(first + count, w * OWNED + OWNED)
    return jnp.maximum(high - low, 0)


def plan_kernel(irreps_ref, table_ref):
    def count(at, counts):
        irrep = irreps_ref[at]
        return tuple(counts[g] + (irrep == g).astype(jnp.int32) for g in range(IRREPS))

    counts = lax.fori_loop(0, TILES, count, (jnp.int32(0),) * IRREPS)
    first = jnp.int32(0)
    firsts = []
    for g in range(IRREPS):
        firsts.append(first)
        table_ref[g] = first
        table_ref[IRREPS + g] = counts[g]
        first = first + counts[g]
    for w in range(VIRT):
        best, main = clip_count(firsts[0], counts[0], w), jnp.int32(0)
        for g in range(1, IRREPS):
            held = clip_count(firsts[g], counts[g], w)
            main = jnp.where(held > best, g, main)
            best = jnp.maximum(held, best)
        table_ref[MAIN + w] = main


def plan(tile_irreps):
    return pl.pallas_call(
        plan_kernel,
        out_shape=jax.ShapeDtypeStruct((32,), jnp.int32),
        in_specs=[pl.BlockSpec(memory_space=pltpu.SMEM)],
        out_specs=pl.BlockSpec(memory_space=pltpu.SMEM),
        name="plan",
    )(tile_irreps)


def position(table_ref, w):
    main = table_ref[MAIN + w]
    first, count = table_ref[main], table_ref[IRREPS + main]
    before = jnp.maximum(first - w * OWNED, 0)
    return main, first, count, before, clip_count(first, count, w)


def pack_kernel(table_ref, own_ref, partner_ref, out_ref, tau_ref):
    for tile in range(TILES):
        columns = pl.ds(tile * TILE, TILE)
        mine = own_ref[:, columns].astype(jnp.float32)
        other = partner_ref[:, columns].astype(jnp.float32)
        tau_ref[tile] = (0.5 * (mine - other)).astype(jnp.bfloat16)
    tau_ref[TILES] = jnp.zeros((ROWS, TILE), jnp.bfloat16)

    @pl.loop(0, VIRT)
    def _(w):
        _, first, count, before, held = position(table_ref, w)
        for slot in range(SECT):
            out_ref[w, slot] = tau_ref[jnp.where(slot < count, first + slot, TILES)]
        for extra in range(EXTRA):
            at = jnp.where(extra < before, extra, extra + held)
            at = jnp.where(at < OWNED, w * OWNED + at, TILES)
            out_ref[w, SECT + extra] = tau_ref[at]


def pack(table, own, partner):
    return pl.pallas_call(
        pack_kernel,
        out_shape=jax.ShapeDtypeStruct((VIRT, SLOTS, ROWS, TILE), jnp.bfloat16),
        in_specs=[pl.BlockSpec(memory_space=pltpu.SMEM)] + [pl.BlockSpec(memory_space=pltpu.VMEM)] * 2,
        out_specs=pl.BlockSpec(memory_space=pltpu.VMEM),
        scratch_shapes=[pltpu.VMEM((TILES + 1, ROWS, TILE), jnp.bfloat16)],
        compiler_params=pltpu.CompilerParams(vmem_limit_bytes=16 << 20),
        name="pack",
    )(table, own, partner)


GROUP = 2
NT = (((1,), (1,)), ((), ()))
NN = (((1,), (0,)), ((), ()))


def tile_at(index, count=1):
    return pl.ds(pl.multiple_of(index * TILE, TILE), count * TILE)


def right_start(first, last_block):
    return jnp.minimum(last_block * OWNED - first, SECT - SIDE)


def ladder_kernel(table_ref, irreps_ref, tau_ref, block_ref, out_ref, held_ref, some_ref, part_ref):
    half, w = table_ref[HALF], table_ref[PLACE]
    main, main_first, _, before, held = position(table_ref, w)
    sign = jnp.where(half == 1, -1.0, 1.0)

    for slot in range(SLOTS):
        for src in range(0, VIRT, 2):
            rows = jnp.concatenate([tau_ref[src, slot], tau_ref[src + 1, slot]], axis=0)
            held_ref[pl.ds(src * ROWS, 2 * ROWS), pl.ds(slot * TILE, TILE)] = rows

    def tau_of(tile):
        inside = w * OWNED + tile - main_first
        outside = SECT + jnp.where(tile < before, tile, tile - held)
        return held_ref[:, tile_at(jnp.where(irreps_ref[w * OWNED + tile] == main, inside, outside))]

    def send(slot, values):
        upper = (values * sign).astype(jnp.bfloat16)
        for dest in range(VIRT):
            rows = upper[dest * ROWS : (dest + 1) * ROWS]
            out_ref[dest, slot] = rows
            out_ref[VIRT + dest, slot] = -rows

    for start in range(0, OWNED, GROUP):
        sums = lax.dot_general(
            block_ref[start * TILE : (start + GROUP) * TILE],
            held_ref[:, : SECT * TILE],
            NT,
            preferred_element_type=jnp.float32,
        )
        for tile in range(GROUP):
            send(start + tile, sums[tile * TILE : (tile + 1) * TILE].T)

    @pl.when(held < OWNED)
    def _():
        @pl.loop(0, IRREPS)
        def _(irrep):
            first, count = table_ref[irrep], table_ref[IRREPS + irrep]
            low = jnp.maximum(first - w * OWNED, 0)
            size = clip_count(first, count, w)

            @pl.when((irrep != main) & (size > 0))
            def _():
                column = w * OWNED + low - first
                start = jnp.minimum(column, SECT - SIDE)
                row = jnp.minimum(low, OWNED - SIDE)
                some_ref[...] = jnp.zeros_like(some_ref)

                @pl.loop(0, size)
                def _(at):
                    some_ref[:, tile_at(column - start + at)] = tau_of(low + at)

                part_ref[...] = lax.dot_general(
                    some_ref[:, : SIDE * TILE],
                    block_ref[tile_at(row, SIDE), tile_at(start, SIDE)],
                    NT,
                    preferred_element_type=jnp.float32,
                )

                @pl.loop(0, size)
                def _(at):
                    send(low + at, part_ref[:, tile_at(low - row + at)])

    def side(slot, edge, is_left):
        irrep = irreps_ref[w * OWNED + edge]
        first, count = table_ref[irrep], table_ref[IRREPS + irrep]
        block = (first if is_left else first + count - 1) // OWNED

        @pl.when((block != w) & (table_ref[MAIN + block] != irrep))
        def _():
            for tile in range(OWNED):
                inside = irreps_ref[w * OWNED + tile] == irrep

                @pl.when(inside)
                def _():
                    some_ref[:, tile * TILE : (tile + 1) * TILE] = tau_of(tile)

                @pl.when(jnp.logical_not(inside))
                def _():
                    some_ref[:, tile * TILE : (tile + 1) * TILE] = jnp.zeros((VIRT * ROWS, TILE), jnp.bfloat16)

            at = 0 if is_left else right_start(first, block)
            part_ref[...] = lax.dot_general(
                some_ref[...], block_ref[:, tile_at(at, SIDE)], NN, preferred_element_type=jnp.float32
            )
            for tile in range(SIDE):
                send(slot + tile, part_ref[:, tile * TILE : (tile + 1) * TILE])

    side(OWNED, 0, True)
    side(OWNED + SIDE, OWNED - 1, False)


def ladder(table, tile_irreps, taken, blocks):
    rows = VIRT * ROWS
    return pl.pallas_call(
        ladder_kernel,
        out_shape=jax.ShapeDtypeStruct((2 * VIRT, OUT_SLOTS, ROWS, TILE), jnp.bfloat16),
        in_specs=[pl.BlockSpec(memory_space=pltpu.SMEM)] * 2 + [pl.BlockSpec(memory_space=pltpu.VMEM)] * 2,
        out_specs=pl.BlockSpec(memory_space=pltpu.VMEM),
        scratch_shapes=[
            pltpu.VMEM((rows, SLOTS * TILE), jnp.bfloat16),
            pltpu.VMEM((rows, OWNED * TILE), jnp.bfloat16),
            pltpu.VMEM((rows, SIDE * TILE), jnp.float32),
        ],
        compiler_params=pltpu.CompilerParams(vmem_limit_bytes=40 << 20),
        cost_estimate=pl.CostEstimate(
            flops=2 * rows * SECT * TILE * OWNED * TILE, bytes_accessed=16 << 20, transcendentals=0
        ),
        name="ladder",
    )(table, tile_irreps, taken, blocks)


def collect_kernel(table_ref, irreps_ref, taken_ref, out_ref):
    @pl.loop(0, VIRT)
    def _(w):
        for tile in range(OWNED):
            both = [taken_ref[half * VIRT + w, tile] for half in range(2)]
            out_ref[:, tile_at(w * OWNED + tile)] = jnp.concatenate(both, axis=0)
        main, _, _, _, held = position(table_ref, w)

        @pl.when(held < OWNED)
        def _():
            @pl.loop(0, OWNED)
            def _(tile):
                at = w * OWNED + tile
                irrep = irreps_ref[at]

                @pl.when(irrep != main)
                def _():
                    first = table_ref[irrep]
                    left_block = first // OWNED
                    right_block = (first + table_ref[IRREPS + irrep] - 1) // OWNED
                    on_left = w == left_block
                    low = jnp.where(on_left, left_block + 1, left_block)
                    high = jnp.where(on_left, right_block + 1, right_block)
                    slot = jnp.where(
                        on_left,
                        OWNED + at - first,
                        OWNED + SIDE + at - first - right_start(first, right_block),
                    )
                    both = []
                    for half in range(2):
                        total = lax.fori_loop(
                            low,
                            high,
                            lambda v, total: total + taken_ref[half * VIRT + v, slot].astype(jnp.float32),
                            taken_ref[half * VIRT + w, tile].astype(jnp.float32),
                        )
                        both.append(total.astype(jnp.bfloat16))
                    out_ref[:, tile_at(at)] = jnp.concatenate(both, axis=0)


def collect(table, tile_irreps, taken):
    return pl.pallas_call(
        collect_kernel,
        out_shape=jax.ShapeDtypeStruct((2 * ROWS, TILES * TILE), jnp.bfloat16),
        in_specs=[pl.BlockSpec(memory_space=pltpu.SMEM)] * 2 + [pl.BlockSpec(memory_space=pltpu.VMEM)],
        out_specs=pl.BlockSpec(memory_space=pltpu.VMEM),
        compiler_params=pltpu.CompilerParams(vmem_limit_bytes=16 << 20),
        name="collect",
    )(table, tile_irreps, taken)


def on_device(amplitudes, tile_irreps, ladder_blocks):
    half = lax.axis_index("half")
    sent = lax.dynamic_slice_in_dim(amplitudes, (1 - half) * ROWS, ROWS, 0)
    own = lax.dynamic_slice_in_dim(amplitudes, half * ROWS, ROWS, 0)
    partner = lax.ppermute(sent, "half", [(0, 1), (1, 0)])
    place = jnp.stack([half, lax.axis_index("virt")]).astype(jnp.int32)
    table = jnp.concatenate([plan(tile_irreps), place])
    packed = pack(table, own, partner)
    taken = lax.all_to_all(packed, "virt", split_axis=0, concat_axis=0, tiled=True)
    sums = ladder(table, tile_irreps, taken, ladder_blocks)
    taken = lax.all_to_all(sums, ("half", "virt"), split_axis=0, concat_axis=0, tiled=True)
    return collect(table, tile_irreps, taken)


def solution(mesh):
    pairs, virt = mesh.devices.shape
    split = Mesh(mesh.devices.reshape(2, pairs // 2, virt), ("half", "quarter", "virt"))
    rows = P(("half", "quarter", "virt"), None)
    return jax.shard_map(
        on_device, mesh=split, in_specs=(rows, P(), P("virt", None)), out_specs=rows, check_vma=False
    )
```

time: 80.6 us -> 77.4 us (0.960)
  local copies, waits for them, and re-layouts: 2.68 us -> 1.07 us
  blocking collectives: 54.4 us -> 53.4 us
    unnamed x8 -> x2, local copies, waits for them, and re-layouts: 1.71 us -> 0.01 us
    all_to_all x1, blocking collectives: 23.2 us -> 22.3 us  [on_device(): lax.all_to_all(sums, ('half', 'virt'), split_axis=0, concat_axis=0, tiled...]
  transfers between devices with their start and end apart: 1 -> 1, of which waited for: 1 -> 1; matrix products, arithmetic and copies ran while one was open for 0% -> 1% of each run, Pallas kernels for 4% -> 4%
where the time goes in v2:
time: 77.4 us; the launch traced here: 77.2 us
  blocking collectives  53.4 us (69%)
  Pallas kernels  16 us (21%)
  starting transfers between devices  3.36 us (4%)
  waiting for transfers between devices  2.59 us (3%)
  local copies, waits for them, and re-layouts  1.07 us (1%)
    all_to_all x1, blocking collectives, on_device(): lax.all_to_all(packed, 'virt', split_axis=0, concat_axis=0, tiled=True)  31.1 us
    all_to_all x1, blocking collectives, on_device(): lax.all_to_all(sums, ('half', 'virt'), split_axis=0, concat_axis=0, tiled...  22.3 us
    pallas_call x1, Pallas kernels, ladder(): pl.pallas_call(ladder_kernel, out_shape=jax.ShapeDtypeStruct((2 * VIRT, O...  8.75 us
    ppermute x1, starting transfers between devices, on_device(): partner = lax.ppermute(sent, 'half', [(0, 1), (1, 0)])  3.36 us
    pallas_call x1, Pallas kernels, plan(): pl.pallas_call(plan_kernel, out_shape=jax.ShapeDtypeStruct((32,), jnp.int...  2.99 us
    ppermute x1, waiting for transfers between devices, on_device(): partner = lax.ppermute(sent, 'half', [(0, 1), (1, 0)])  2.59 us
    pallas_call x1, Pallas kernels, collect(): pl.pallas_call(collect_kernel, out_shape=jax.ShapeDtypeStruct((2 * ROWS,...  2.26 us
    pallas_call x1, Pallas kernels, pack(): pl.pallas_call(pack_kernel, out_shape=jax.ShapeDtypeStruct((VIRT, SLOTS,...  2.02 us
  transfers between devices with their start and end apart: 1, of which 1 were waited for; matrix products, arithmetic and copies ran while one was open for 1% of the time, Pallas kernels for 4%

profile of v2, /device:TPU:0, one launch (start us, length us, event | category | flops | bytes accessed | tf_op | source)
XLA Modules:
  0.0 77.2 jit_solution(17663014794304644240)
XLA Ops:
  0.0 1.1 %constant_dynamic-slice_fusion = (bf16[8,16384]{1,0:T(8,128)(2,1)S(1)}, bf16[8,16384]{1,0:T(8,128)(2,1)S(1)}) fusion(bf16[16,16384]{1,0:T(8,128)(2,1)} %param.3, s32[]{:T(128)S(6)} %select_n.7, s32[]{:T(128)S(6)} %select_n.6), kind=kLoop, calls=%fused_computation.1 | loop fusion | bytes 1048584 | tf_op jit(solution)/shard_map/dynamic_slice | solution.py:277
  1.1 3.4 %collective-permute-start = (bf16[8,16384]{1,0:T(8,128)(2,1)S(1)}, bf16[8,16384]{1,0:T(8,128)(2,1)S(1)}, u32[]{:S(2)}, u32[]{:S(2)}) collective-permute-start(bf16[8,16384]{1,0:T(8,128)(2,1)S(1)} %get-tuple-element.5), channel_id=1, source_target_pairs={{0,64},{64,0},{1,65},{65,1},{2,66},{66,2},{3,67},{67,3},{4,68},{68... | collective-permute-start | bytes 786440 | tf_op jit(solution)/shard_map/ppermute | solution.py:279
  4.4 3.0 %plan.1 = s32[32]{0:T(128)} custom-call(s32[128]{0:T(128)} %irreps_ref.5), custom_call_target="tpu_custom_call" | custom-call | tf_op jit(solution)/shard_map/plan/pallas_call | solution.py:53
  7.4 0.7 pad_add_fusion.table_ref
  8.1 2.6 %collective-permute-done.partner_ref = bf16[8,16384]{1,0:T(8,128)(2,1)S(1)} collective-permute-done((bf16[8,16384]{1,0:T(8,128)(2,1)S(1)}, bf16[8,16384]{1,0:T(8,128)(2,1)S(1)}, u32[]{:S(2)}, u32[]{:S(2)}) %collective-permute-start) | collective-permute-done | bytes 262176 | tf_op jit(solution)/shard_map/ppermute | solution.py:279
  10.7 2.0 %pack.1 = bf16[16,53,8,128]{3,2,1,0:T(8,128)(2,1)S(1)} custom-call(s32[34]{0:T(128)S(1)} %pad_add_fusion.table_ref, bf16[8,16384]{1,0:T(8,128)(2,1)S(1)} %get-tuple-element.6.own_ref, bf16[8,16384]{1,0:T(8,128)(2,1)S(1)} %collective-permute-done.partner_ref), custom_call_target="tpu_custom_call" | custom-call | tf_op jit(solution)/shard_map/pack/pallas_call | solution.py:89
  12.8 0.0 copy-start
  12.8 31.1 %all_to_all.10.tau_ref = bf16[16,53,8,128]{3,2,1,0:T(8,128)(2,1)S(1)} all-to-all(bf16[16,53,8,128]{3,2,1,0:T(8,128)(2,1)S(1)} %pack.1), channel_id=1, replica_groups=mesh['half'=2,'quarter'=4,'virt'=16] {'virt'}, dimensions={0} | all-to-all | bytes 3473408 | tf_op jit(solution)/shard_map/all_to_all | solution.py:283
  43.9 0.0 copy-done
  43.9 8.7 %ladder.1 = bf16[32,16,8,128]{3,2,1,0:T(8,128)(2,1)S(1)} custom-call(s32[34]{0:T(128)S(1)} %pad_add_fusion.table_ref, s32[128]{0:T(128)S(1)} %copy-done, bf16[16,53,8,128]{3,2,1,0:T(8,128)(2,1)S(1)} %all_to_all.10.tau_ref, bf16[1024,6144]{1,0:T(8,128)(2,1)} %block_ref.1), custom_call_target="tpu_custom_call" | custom-call | flops 1610612736 | bytes 16777216 | tf_op jit(solution)/shard_map/ladder/pallas_call | solution.py:206
  52.7 22.3 %all_to_all.11.taken_ref = bf16[32,16,8,128]{3,2,1,0:T(8,128)(2,1)S(1)} all-to-all(bf16[32,16,8,128]{3,2,1,0:T(8,128)(2,1)S(1)} %ladder.1), channel_id=1, replica_groups=mesh['half'=2,'quarter'=4,'virt'=16] {'half','virt'}, dimensions={0} | all-to-all | bytes 2097152 | tf_op jit(solution)/shard_map/all_to_all | solution.py:285
  75.0 2.3 %collect.1 = bf16[16,16384]{1,0:T(8,128)(2,1)} custom-call(s32[34]{0:T(128)S(1)} %pad_add_fusion.table_ref, s32[128]{0:T(128)S(1)} %copy-done, bf16[32,16,8,128]{3,2,1,0:T(8,128)(2,1)S(1)} %all_to_all.11.taken_ref), custom_call_target="tpu_custom_call" | custom-call | tf_op jit(solution)/shard_map/collect/pallas_call | solution.py:265
Async XLA Ops:
  1.1 9.7 %collective-permute-start = (bf16[8,16384]{1,0:T(8,128)(2,1)S(1)}, bf16[8,16384]{1,0:T(8,128)(2,1)S(1)}, u32[]{:S(2)}, u32[]{:S(2)}) collective-permute-start(bf16[8,16384]{1,0:T(8,128)(2,1)S(1)} %get-tuple-element.5), channel_id=1, source_target_pairs={{0,64},{64,0},{1,65},{65,1},{2,66},{66,2},{3,67},{67,3},{4,68},{68... | collective-permute-start | bytes 786440 | tf_op jit(solution)/shard_map/ppermute | solution.py:279
  12.8 31.2 %copy-start = (s32[128]{0:T(128)S(1)}, s32[128]{0:T(128)}, u32[]{:S(2)}) copy-start(s32[128]{0:T(128)} %irreps_ref.5) | copy-start | bytes 1540

commit v3 on v2

--- a/solution.py
+++ b/solution.py
@@ -27,7 +27,10 @@
     return jnp.maximum(high - low, 0)
 
 
-def plan_kernel(irreps_ref, table_ref):
+def plan_kernel(irreps_ref, blocks_ref, table_ref, near_ref, copied):
+    copy = pltpu.make_async_copy(blocks_ref, near_ref, copied)
+    copy.start()
+
     def count(at, counts):
         irrep = irreps_ref[at]
         return tuple(counts[g] + (irrep == g).astype(jnp.int32) for g in range(IRREPS))
@@ -47,16 +50,20 @@
             main = jnp.where(held > best, g, main)
             best = jnp.maximum(held, best)
         table_ref[MAIN + w] = main
-
-
-def plan(tile_irreps):
+    copy.wait()
+
+
+def plan(tile_irreps, blocks):
     return pl.pallas_call(
         plan_kernel,
-        out_shape=jax.ShapeDtypeStruct((32,), jnp.int32),
-        in_specs=[pl.BlockSpec(memory_space=pltpu.SMEM)],
-        out_specs=pl.BlockSpec(memory_space=pltpu.SMEM),
+        out_shape=(jax.ShapeDtypeStruct((32,), jnp.int32), jax.ShapeDtypeStruct(blocks.shape, blocks.dtype)),
+        in_specs=[pl.BlockSpec(memory_space=pltpu.SMEM), pl.BlockSpec(memory_space=pltpu.HBM)],
+        out_specs=(pl.BlockSpec(memory_space=pltpu.SMEM), pl.BlockSpec(memory_space=pltpu.VMEM)),
+        scratch_shapes=[pltpu.SemaphoreType.DMA],
+        compiler_params=pltpu.CompilerParams(vmem_limit_bytes=37 << 20),
+        cost_estimate=pl.CostEstimate(flops=0, bytes_accessed=2 * blocks.size * 2, transcendentals=0),
         name="plan",
-    )(tile_irreps)
+    )(tile_irreps, blocks)
 
 
 def position(table_ref, w):
@@ -213,7 +220,7 @@
             pltpu.VMEM((rows, OWNED * TILE), jnp.bfloat16),
             pltpu.VMEM((rows, SIDE * TILE), jnp.float32),
         ],
-        compiler_params=pltpu.CompilerParams(vmem_limit_bytes=40 << 20),
+        compiler_params=pltpu.CompilerParams(vmem_limit_bytes=24 << 20),
         cost_estimate=pl.CostEstimate(
             flops=2 * rows * SECT * TILE * OWNED * TILE, bytes_accessed=16 << 20, transcendentals=0
         ),
@@ -278,10 +285,11 @@
     own = lax.dynamic_slice_in_dim(amplitudes, half * ROWS, ROWS, 0)
     partner = lax.ppermute(sent, "half", [(0, 1), (1, 0)])
     place = jnp.stack([half, lax.axis_index("virt")]).astype(jnp.int32)
-    table = jnp.concatenate([plan(tile_irreps), place])
+    table, near = plan(tile_irreps, ladder_blocks)
+    table = jnp.concatenate([table, place])
     packed = pack(table, own, partner)
     taken = lax.all_to_all(packed, "virt", split_axis=0, concat_axis=0, tiled=True)
-    sums = ladder(table, tile_irreps, taken, ladder_blocks)
+    sums = ladder(table, tile_irreps, taken, near)
     taken = lax.all_to_all(sums, ("half", "virt"), split_axis=0, concat_axis=0, tiled=True)
     return collect(table, tile_irreps, taken)
 

time: 77.4 us -> 73.5 us (0.950)
  waiting for transfers between devices: 2.59 us -> 0.01 us
  Pallas kernels: 16 us -> 14.1 us
    pallas_call x1, Pallas kernels: 8.75 us -> 4.16 us  [ladder(): pl.pallas_call(ladder_kernel, out_shape=jax.ShapeDtypeStruct((2 * VIRT, O...]
    pallas_call x1, Pallas kernels: 2.99 us -> 5.72 us  [plan(): pl.pallas_call(plan_kernel, out_shape=(jax.ShapeDtypeStruct((32,), jnp.in...]
    ppermute x1, waiting for transfers between devices: 2.59 us -> 0.01 us  [on_device(): partner = lax.ppermute(sent, 'half', [(0, 1), (1, 0)])]
  transfers between devices with their start and end apart: 1 -> 1, of which waited for: 1 -> 0; matrix products, arithmetic and copies ran while one was open for 1% -> 0% of each run, Pallas kernels for 4% -> 8%
where the time goes in v3:
time: 73.5 us; the launch traced here: 73.1 us
  blocking collectives  53.8 us (73%)
  Pallas kernels  14.1 us (19%)
  starting transfers between devices  3.36 us (5%)
  local copies, waits for them, and re-layouts  1.73 us (2%)
    all_to_all x1, blocking collectives, on_device(): lax.all_to_all(packed, 'virt', split_axis=0, concat_axis=0, tiled=True)  31.7 us
    all_to_all x1, blocking collectives, on_device(): lax.all_to_all(sums, ('half', 'virt'), split_axis=0, concat_axis=0, tiled...  22.1 us
    pallas_call x1, Pallas kernels, plan(): pl.pallas_call(plan_kernel, out_shape=(jax.ShapeDtypeStruct((32,), jnp.in...  5.72 us
    pallas_call x1, Pallas kernels, ladder(): pl.pallas_call(ladder_kernel, out_shape=jax.ShapeDtypeStruct((2 * VIRT, O...  4.16 us
    ppermute x1, starting transfers between devices, on_device(): partner = lax.ppermute(sent, 'half', [(0, 1), (1, 0)])  3.36 us
    pallas_call x1, Pallas kernels, collect(): pl.pallas_call(collect_kernel, out_shape=jax.ShapeDtypeStruct((2 * ROWS,...  2.2 us
    pallas_call x1, Pallas kernels, pack(): pl.pallas_call(pack_kernel, out_shape=jax.ShapeDtypeStruct((VIRT, SLOTS,...  2.02 us
  transfers between devices with their start and end apart: 1, of which 0 were waited for; matrix products, arithmetic and copies ran while one was open for 0% of the time, Pallas kernels for 8%

profile of v3, /device:TPU:0, one launch (start us, length us, event | category | flops | bytes accessed | tf_op | source)
XLA Modules:
  0.0 73.1 jit_solution(16755691166592089046)
XLA Ops:
  0.0 0.0 copy-start.1
  0.0 1.1 %constant_dynamic-slice_fusion = (bf16[8,16384]{1,0:T(8,128)(2,1)S(1)}, bf16[8,16384]{1,0:T(8,128)(2,1)S(1)}) fusion(bf16[16,16384]{1,0:T(8,128)(2,1)} %param.3, s32[]{:T(128)S(6)} %select_n.7, s32[]{:T(128)S(6)} %select_n.6), kind=kLoop, calls=%fused_computation.1 | loop fusion | bytes 1048584 | tf_op jit(solution)/shard_map/dynamic_slice | solution.py:284
  1.1 3.4 %collective-permute-start = (bf16[8,16384]{1,0:T(8,128)(2,1)S(1)}, bf16[8,16384]{1,0:T(8,128)(2,1)S(1)}, u32[]{:S(2)}, u32[]{:S(2)}) collective-permute-start(bf16[8,16384]{1,0:T(8,128)(2,1)S(1)} %get-tuple-element.9), channel_id=1, source_target_pairs={{0,64},{64,0},{1,65},{65,1},{2,66},{66,2},{3,67},{67,3},{4,68},{68... | collective-permute-start | bytes 786440 | tf_op jit(solution)/shard_map/ppermute | solution.py:286
  4.4 0.0 copy-start
  4.4 0.7 copy-done
  5.1 5.7 %plan.1 = (s32[32]{0:T(128)S(1)}, bf16[1024,6144]{1,0:T(8,128)(2,1)S(1)}) custom-call(s32[128]{0:T(128)S(1)} %copy-done, bf16[1024,6144]{1,0:T(8,128)(2,1)} %blocks_ref.1), custom_call_target="tpu_custom_call" | custom-call | bytes 25165824 | tf_op jit(solution)/shard_map/plan/pallas_call | solution.py:57
  10.8 0.1 pad_add_fusion.table_ref
  10.9 0.0 collective-permute-done.partner_ref
  10.9 2.0 %pack.1 = bf16[16,53,8,128]{3,2,1,0:T(8,128)(2,1)S(1)} custom-call(s32[34]{0:T(128)S(1)} %pad_add_fusion.table_ref, bf16[8,16384]{1,0:T(8,128)(2,1)S(1)} %get-tuple-element.10.own_ref, bf16[8,16384]{1,0:T(8,128)(2,1)S(1)} %collective-permute-done.partner_ref), custom_call_target="tpu_custom_call" | custom-call | tf_op jit(solution)/shard_map/pack/pallas_call | solution.py:96
  12.9 31.7 %all_to_all.10.tau_ref = bf16[16,53,8,128]{3,2,1,0:T(8,128)(2,1)S(1)} all-to-all(bf16[16,53,8,128]{3,2,1,0:T(8,128)(2,1)S(1)} %pack.1), channel_id=1, replica_groups=mesh['half'=2,'quarter'=4,'virt'=16] {'virt'}, dimensions={0} | all-to-all | bytes 3473408 | tf_op jit(solution)/shard_map/all_to_all | solution.py:291
  44.6 0.0 copy-done.1
  44.6 4.2 %ladder.1 = bf16[32,16,8,128]{3,2,1,0:T(8,128)(2,1)S(1)} custom-call(s32[34]{0:T(128)S(1)} %pad_add_fusion.table_ref, s32[128]{0:T(128)S(1)} %copy-done.1, bf16[16,53,8,128]{3,2,1,0:T(8,128)(2,1)S(1)} %all_to_all.10.tau_ref, bf16[1024,6144]{1,0:T(8,128)(2,1)S(1)} %get-tuple-element.8.block_ref), custom_call_target="tpu_custom_call" | custom-call | flops 1610612736 | bytes 16777216 | tf_op jit(solution)/shard_map/ladder/pallas_call | solution.py:213
  48.8 22.1 %all_to_all.11.taken_ref = bf16[32,16,8,128]{3,2,1,0:T(8,128)(2,1)S(1)} all-to-all(bf16[32,16,8,128]{3,2,1,0:T(8,128)(2,1)S(1)} %ladder.1), channel_id=1, replica_groups=mesh['half'=2,'quarter'=4,'virt'=16] {'half','virt'}, dimensions={0} | all-to-all | bytes 2097152 | tf_op jit(solution)/shard_map/all_to_all | solution.py:293
  70.9 2.2 %collect.1 = bf16[16,16384]{1,0:T(8,128)(2,1)} custom-call(s32[34]{0:T(128)S(1)} %pad_add_fusion.table_ref, s32[128]{0:T(128)S(1)} %copy-done.1, bf16[32,16,8,128]{3,2,1,0:T(8,128)(2,1)S(1)} %all_to_all.11.taken_ref), custom_call_target="tpu_custom_call" | custom-call | tf_op jit(solution)/shard_map/collect/pallas_call | solution.py:272
Async XLA Ops:
  0.0 44.6 %copy-start.1 = (s32[128]{0:T(128)S(1)}, s32[128]{0:T(128)}, u32[]{:S(2)}) copy-start(s32[128]{0:T(128)} %irreps_ref.5) | copy-start | bytes 1540
  1.1 9.8 %collective-permute-start = (bf16[8,16384]{1,0:T(8,128)(2,1)S(1)}, bf16[8,16384]{1,0:T(8,128)(2,1)S(1)}, u32[]{:S(2)}, u32[]{:S(2)}) collective-permute-start(bf16[8,16384]{1,0:T(8,128)(2,1)S(1)} %get-tuple-element.9), channel_id=1, source_target_pairs={{0,64},{64,0},{1,65},{65,1},{2,66},{66,2},{3,67},{67,3},{4,68},{68... | collective-permute-start | bytes 786440 | tf_op jit(solution)/shard_map/ppermute | solution.py:286
  4.4 0.7 copy-start

commit v4 on v3

--- a/solution.py
+++ b/solution.py
@@ -79,13 +79,12 @@
         mine = own_ref[:, columns].astype(jnp.float32)
         other = partner_ref[:, columns].astype(jnp.float32)
         tau_ref[tile] = (0.5 * (mine - other)).astype(jnp.bfloat16)
-    tau_ref[TILES] = jnp.zeros((ROWS, TILE), jnp.bfloat16)
+    tau_ref[TILES:] = jnp.zeros((SECT, ROWS, TILE), jnp.bfloat16)
 
     @pl.loop(0, VIRT)
     def _(w):
-        _, first, count, before, held = position(table_ref, w)
-        for slot in range(SECT):
-            out_ref[w, slot] = tau_ref[jnp.where(slot < count, first + slot, TILES)]
+        _, first, _, before, held = position(table_ref, w)
+        out_ref[w, :SECT] = tau_ref[pl.ds(first, SECT)]
         for extra in range(EXTRA):
             at = jnp.where(extra < before, extra, extra + held)
             at = jnp.where(at < OWNED, w * OWNED + at, TILES)
@@ -98,19 +97,21 @@
         out_shape=jax.ShapeDtypeStruct((VIRT, SLOTS, ROWS, TILE), jnp.bfloat16),
         in_specs=[pl.BlockSpec(memory_space=pltpu.SMEM)] + [pl.BlockSpec(memory_space=pltpu.VMEM)] * 2,
         out_specs=pl.BlockSpec(memory_space=pltpu.VMEM),
-        scratch_shapes=[pltpu.VMEM((TILES + 1, ROWS, TILE), jnp.bfloat16)],
+        scratch_shapes=[pltpu.VMEM((TILES + SECT, ROWS, TILE), jnp.bfloat16)],
         compiler_params=pltpu.CompilerParams(vmem_limit_bytes=16 << 20),
         name="pack",
     )(table, own, partner)
 
 
 GROUP = 2
+SHORT = 32
 NT = (((1,), (1,)), ((), ()))
 NN = (((1,), (0,)), ((), ()))
 
 
 def tile_at(index, count=1):
-    return pl.ds(pl.multiple_of(index * TILE, TILE), count * TILE)
+    start = index * TILE if isinstance(index, int) else pl.multiple_of(index * TILE, TILE)
+    return pl.ds(start, count * TILE)
 
 
 def right_start(first, last_block):
@@ -119,7 +120,7 @@
 
 def ladder_kernel(table_ref, irreps_ref, tau_ref, block_ref, out_ref, held_ref, some_ref, part_ref):
     half, w = table_ref[HALF], table_ref[PLACE]
-    main, main_first, _, before, held = position(table_ref, w)
+    main, main_first, main_count, before, held = position(table_ref, w)
     sign = jnp.where(half == 1, -1.0, 1.0)
 
     for slot in range(SLOTS):
@@ -136,18 +137,26 @@
         upper = (values * sign).astype(jnp.bfloat16)
         for dest in range(VIRT):
             rows = upper[dest * ROWS : (dest + 1) * ROWS]
-            out_ref[dest, slot] = rows
-            out_ref[VIRT + dest, slot] = -rows
-
-    for start in range(0, OWNED, GROUP):
-        sums = lax.dot_general(
-            block_ref[start * TILE : (start + GROUP) * TILE],
-            held_ref[:, : SECT * TILE],
-            NT,
-            preferred_element_type=jnp.float32,
-        )
-        for tile in range(GROUP):
-            send(start + tile, sums[tile * TILE : (tile + 1) * TILE].T)
+            out_ref[dest, :, tile_at(slot)] = rows
+            out_ref[VIRT + dest, :, tile_at(slot)] = -rows
+
+    def multiply(depth):
+        @pl.loop(main_count, depth)
+        def _(slot):
+            held_ref[:, tile_at(slot)] = jnp.zeros((VIRT * ROWS, TILE), jnp.bfloat16)
+
+        for start in range(0, OWNED, GROUP):
+            sums = lax.dot_general(
+                block_ref[start * TILE : (start + GROUP) * TILE, : depth * TILE],
+                held_ref[:, : depth * TILE],
+                NT,
+                preferred_element_type=jnp.float32,
+            )
+            for tile in range(GROUP):
+                send(start + tile, sums[tile * TILE : (tile + 1) * TILE].T)
+
+    pl.when(main_count <= SHORT)(lambda: multiply(SHORT))
+    pl.when(main_count > SHORT)(lambda: multiply(SECT))
 
     @pl.when(held < OWNED)
     def _():
@@ -212,7 +221,7 @@
     rows = VIRT * ROWS
     return pl.pallas_call(
         ladder_kernel,
-        out_shape=jax.ShapeDtypeStruct((2 * VIRT, OUT_SLOTS, ROWS, TILE), jnp.bfloat16),
+        out_shape=jax.ShapeDtypeStruct((2 * VIRT, ROWS, OUT_SLOTS * TILE), jnp.bfloat16),
         in_specs=[pl.BlockSpec(memory_space=pltpu.SMEM)] * 2 + [pl.BlockSpec(memory_space=pltpu.VMEM)] * 2,
         out_specs=pl.BlockSpec(memory_space=pltpu.VMEM),
         scratch_shapes=[
@@ -228,55 +237,104 @@
     )(table, tile_irreps, taken, blocks)
 
 
-def collect_kernel(table_ref, irreps_ref, taken_ref, out_ref):
+def collect_kernel(table_ref, taken_ref, out_ref, mixed_ref, total_ref, sent, mixed_sent):
+    def copy(w, half):
+        return pltpu.make_async_copy(
+            taken_ref.at[half * VIRT + w, :, : OWNED * TILE], out_ref.at[half, :, tile_at(w * OWNED, OWNED)], sent
+        )
+
+    def mixed_copy(w, half):
+        return pltpu.make_async_copy(
+            mixed_ref.at[half * VIRT + w], out_ref.at[half, :, tile_at(w * OWNED, OWNED)], mixed_sent
+        )
+
+    def is_mixed(w):
+        return position(table_ref, w)[4] < OWNED
+
     @pl.loop(0, VIRT)
     def _(w):
-        for tile in range(OWNED):
-            both = [taken_ref[half * VIRT + w, tile] for half in range(2)]
-            out_ref[:, tile_at(w * OWNED + tile)] = jnp.concatenate(both, axis=0)
-        main, _, _, _, held = position(table_ref, w)
-
-        @pl.when(held < OWNED)
-        def _():
-            @pl.loop(0, OWNED)
-            def _(tile):
-                at = w * OWNED + tile
-                irrep = irreps_ref[at]
-
-                @pl.when(irrep != main)
+        mixed = is_mixed(w)
+
+        @pl.when(jnp.logical_not(mixed))
+        def _():
+            for half in range(2):
+                copy(w, half).start()
+
+    @pl.loop(0, VIRT)
+    def _(w):
+        @pl.when(is_mixed(w))
+        def _():
+            main = table_ref[MAIN + w]
+            for half in range(2):
+                mixed_ref[half * VIRT + w] = taken_ref[half * VIRT + w, :, : OWNED * TILE]
+
+            @pl.loop(0, IRREPS)
+            def _(irrep):
+                first, count = table_ref[irrep], table_ref[IRREPS + irrep]
+                size = clip_count(first, count, w)
+
+                @pl.when((irrep != main) & (size > 0))
                 def _():
-                    first = table_ref[irrep]
-                    left_block = first // OWNED
-                    right_block = (first + table_ref[IRREPS + irrep] - 1) // OWNED
+                    left_block, right_block = first // OWNED, (first + count - 1) // OWNED
                     on_left = w == left_block
                     low = jnp.where(on_left, left_block + 1, left_block)
                     high = jnp.where(on_left, right_block + 1, right_block)
-                    slot = jnp.where(
-                        on_left,
-                        OWNED + at - first,
-                        OWNED + SIDE + at - first - right_start(first, right_block),
-                    )
-                    both = []
+                    tile = jnp.maximum(first - w * OWNED, 0)
+                    offset = jnp.where(on_left, 0, w * OWNED - first - right_start(first, right_block))
+                    slots = tile_at(jnp.where(on_left, OWNED, OWNED + SIDE), SIDE)
+
+                    def add(v, totals):
+                        return tuple(
+                            totals[half] + taken_ref[half * VIRT + v, :, slots].astype(jnp.float32) for half in range(2)
+                        )
+
+                    zeros = jnp.zeros((ROWS, SIDE * TILE), jnp.float32)
+                    totals = lax.fori_loop(low, high, add, (zeros, zeros))
                     for half in range(2):
-                        total = lax.fori_loop(
-                            low,
-                            high,
-                            lambda v, total: total + taken_ref[half * VIRT + v, slot].astype(jnp.float32),
-                            taken_ref[half * VIRT + w, tile].astype(jnp.float32),
-                        )
-                        both.append(total.astype(jnp.bfloat16))
-                    out_ref[:, tile_at(at)] = jnp.concatenate(both, axis=0)
-
-
-def collect(table, tile_irreps, taken):
-    return pl.pallas_call(
+                        total_ref[half] = totals[half]
+
+                    @pl.loop(0, size)
+                    def _(at):
+                        columns = tile_at(tile + at)
+                        for half in range(2):
+                            own = taken_ref[half * VIRT + w, :, columns].astype(jnp.float32)
+                            total = own + total_ref[half, :, tile_at(offset + at)]
+                            mixed_ref[half * VIRT + w, :, columns] = total.astype(jnp.bfloat16)
+
+            for half in range(2):
+                mixed_copy(w, half).start()
+
+    @pl.loop(0, VIRT)
+    def _(w):
+        mixed = is_mixed(w)
+
+        @pl.when(mixed)
+        def _():
+            for half in range(2):
+                mixed_copy(w, half).wait()
+
+        @pl.when(jnp.logical_not(mixed))
+        def _():
+            for half in range(2):
+                copy(w, half).wait()
+
+
+def collect(table, taken):
+    out = pl.pallas_call(
         collect_kernel,
-        out_shape=jax.ShapeDtypeStruct((2 * ROWS, TILES * TILE), jnp.bfloat16),
-        in_specs=[pl.BlockSpec(memory_space=pltpu.SMEM)] * 2 + [pl.BlockSpec(memory_space=pltpu.VMEM)],
-        out_specs=pl.BlockSpec(memory_space=pltpu.VMEM),
+        out_shape=jax.ShapeDtypeStruct((2, ROWS, TILES * TILE), jnp.bfloat16),
+        in_specs=[pl.BlockSpec(memory_space=pltpu.SMEM), pl.BlockSpec(memory_space=pltpu.VMEM)],
+        out_specs=pl.BlockSpec(memory_space=pltpu.HBM),
+        scratch_shapes=[
+            pltpu.VMEM((2 * VIRT, ROWS, OWNED * TILE), jnp.bfloat16),
+            pltpu.VMEM((2, ROWS, SIDE * TILE), jnp.float32),
+            pltpu.SemaphoreType.DMA,
+            pltpu.SemaphoreType.DMA,
+        ],
         compiler_params=pltpu.CompilerParams(vmem_limit_bytes=16 << 20),
         name="collect",
-    )(table, tile_irreps, taken)
+    )(table, taken)
+    return out.reshape(2 * ROWS, TILES * TILE)
 
 
 def on_device(amplitudes, tile_irreps, ladder_blocks):
@@ -291,7 +349,7 @@
     taken = lax.all_to_all(packed, "virt", split_axis=0, concat_axis=0, tiled=True)
     sums = ladder(table, tile_irreps, taken, near)
     taken = lax.all_to_all(sums, ("half", "virt"), split_axis=0, concat_axis=0, tiled=True)
-    return collect(table, tile_irreps, taken)
+    return collect(table, taken)
 
 
 def solution(mesh):

time: 73.5 us -> 71.9 us (0.978)
  Pallas kernels: 14.1 us -> 13.1 us
  blocking collectives: 53.8 us -> 52.8 us
    pallas_call x1, Pallas kernels: 2.02 us -> 1.03 us  [pack(): pl.pallas_call(pack_kernel, out_shape=jax.ShapeDtypeStruct((VIRT, SLOTS,...]
    all_to_all x1, blocking collectives: 22.1 us -> 21.1 us  [on_device(): lax.all_to_all(sums, ('half', 'virt'), split_axis=0, concat_axis=0, tiled...]
where the time goes in v4:
time: 71.9 us; the launch traced here: 71.1 us
  blocking collectives  52.8 us (73%)
  Pallas kernels  13.1 us (18%)
  starting transfers between devices  3.36 us (5%)
  local copies, waits for them, and re-layouts  1.73 us (2%)
    all_to_all x1, blocking collectives, on_device(): lax.all_to_all(packed, 'virt', split_axis=0, concat_axis=0, tiled=True)  31.7 us
    all_to_all x1, blocking collectives, on_device(): lax.all_to_all(sums, ('half', 'virt'), split_axis=0, concat_axis=0, tiled...  21.1 us
    pallas_call x1, Pallas kernels, plan(): pl.pallas_call(plan_kernel, out_shape=(jax.ShapeDtypeStruct((32,), jnp.in...  5.72 us
    pallas_call x1, Pallas kernels, ladder(): pl.pallas_call(ladder_kernel, out_shape=jax.ShapeDtypeStruct((2 * VIRT, R...  4.41 us
    ppermute x1, starting transfers between devices, on_device(): partner = lax.ppermute(sent, 'half', [(0, 1), (1, 0)])  3.36 us
    pallas_call x1, Pallas kernels, collect(): pl.pallas_call(collect_kernel, out_shape=jax.ShapeDtypeStruct((2, ROWS, T...  1.91 us
  transfers between devices with their start and end apart: 1, of which 0 were waited for; matrix products, arithmetic and copies ran while one was open for 0% of the time, Pallas kernels for 8%

profile of v4, /device:TPU:0, one launch (start us, length us, event | category | flops | bytes accessed | tf_op | source)
XLA Modules:
  0.0 71.1 jit_solution(2313304365047687075)
XLA Ops:
  0.0 0.0 copy-start.1
  0.0 1.1 %constant_dynamic-slice_fusion = (bf16[8,16384]{1,0:T(8,128)(2,1)S(1)}, bf16[8,16384]{1,0:T(8,128)(2,1)S(1)}) fusion(bf16[16,16384]{1,0:T(8,128)(2,1)} %param.3, s32[]{:T(128)S(6)} %select_n.7, s32[]{:T(128)S(6)} %select_n.6), kind=kLoop, calls=%fused_computation.1 | loop fusion | bytes 1048584 | tf_op jit(solution)/shard_map/dynamic_slice | solution.py:342
  1.1 3.4 %collective-permute-start = (bf16[8,16384]{1,0:T(8,128)(2,1)S(1)}, bf16[8,16384]{1,0:T(8,128)(2,1)S(1)}, u32[]{:S(2)}, u32[]{:S(2)}) collective-permute-start(bf16[8,16384]{1,0:T(8,128)(2,1)S(1)} %get-tuple-element.9), channel_id=1, source_target_pairs={{0,64},{64,0},{1,65},{65,1},{2,66},{66,2},{3,67},{67,3},{4,68},{68... | collective-permute-start | bytes 786440 | tf_op jit(solution)/shard_map/ppermute | solution.py:344
  4.4 0.0 copy-start
  4.4 0.7 copy-done
  5.1 5.7 %plan.1 = (s32[32]{0:T(128)S(1)}, bf16[1024,6144]{1,0:T(8,128)(2,1)S(1)}) custom-call(s32[128]{0:T(128)S(1)} %copy-done, bf16[1024,6144]{1,0:T(8,128)(2,1)} %blocks_ref.1), custom_call_target="tpu_custom_call" | custom-call | bytes 25165824 | tf_op jit(solution)/shard_map/plan/pallas_call | solution.py:57
  10.8 0.1 pad_add_fusion.table_ref
  10.9 0.0 collective-permute-done.partner_ref
  10.9 1.0 %pack.1 = bf16[16,53,8,128]{3,2,1,0:T(8,128)(2,1)S(1)} custom-call(s32[34]{0:T(128)S(1)} %pad_add_fusion.table_ref, bf16[8,16384]{1,0:T(8,128)(2,1)S(1)} %get-tuple-element.10.own_ref, bf16[8,16384]{1,0:T(8,128)(2,1)S(1)} %collective-permute-done.partner_ref), custom_call_target="tpu_custom_call" | custom-call | tf_op jit(solution)/shard_map/pack/pallas_call | solution.py:95
  11.9 31.7 %all_to_all.10.tau_ref = bf16[16,53,8,128]{3,2,1,0:T(8,128)(2,1)S(1)} all-to-all(bf16[16,53,8,128]{3,2,1,0:T(8,128)(2,1)S(1)} %pack.1), channel_id=1, replica_groups=mesh['half'=2,'quarter'=4,'virt'=16] {'virt'}, dimensions={0} | all-to-all | bytes 3473408 | tf_op jit(solution)/shard_map/all_to_all | solution.py:349
  43.6 0.0 copy-done.1
  43.6 4.4 %ladder.1 = bf16[32,8,2048]{2,1,0:T(8,128)(2,1)S(1)} custom-call(s32[34]{0:T(128)S(1)} %pad_add_fusion.table_ref, s32[128]{0:T(128)S(1)} %copy-done.1, bf16[16,53,8,128]{3,2,1,0:T(8,128)(2,1)S(1)} %all_to_all.10.tau_ref, bf16[1024,6144]{1,0:T(8,128)(2,1)S(1)} %get-tuple-element.8.block_ref), custom_call_target="tpu_custom_call" | custom-call | flops 1610612736 | bytes 16777216 | tf_op jit(solution)/shard_map/ladder/pallas_call | solution.py:222
  48.1 21.1 %all_to_all.11.taken_ref = bf16[32,8,2048]{2,1,0:T(8,128)(2,1)S(1)} all-to-all(bf16[32,8,2048]{2,1,0:T(8,128)(2,1)S(1)} %ladder.1), channel_id=1, replica_groups=mesh['half'=2,'quarter'=4,'virt'=16] {'half','virt'}, dimensions={0} | all-to-all | bytes 2097152 | tf_op jit(solution)/shard_map/all_to_all | solution.py:351
  69.2 1.9 %collect.1 = bf16[2,8,16384]{2,1,0:T(8,128)(2,1)} custom-call(s32[34]{0:T(128)S(1)} %pad_add_fusion.table_ref, bf16[32,8,2048]{2,1,0:T(8,128)(2,1)S(1)} %all_to_all.11.taken_ref), custom_call_target="tpu_custom_call" | custom-call | tf_op jit(solution)/shard_map/collect/pallas_call | solution.py:323
Async XLA Ops:
  0.0 43.6 %copy-start.1 = (s32[128]{0:T(128)S(1)}, s32[128]{0:T(128)}, u32[]{:S(2)}) copy-start(s32[128]{0:T(128)} %irreps_ref.3) | copy-start | bytes 1540
  1.1 9.8 %collective-permute-start = (bf16[8,16384]{1,0:T(8,128)(2,1)S(1)}, bf16[8,16384]{1,0:T(8,128)(2,1)S(1)}, u32[]{:S(2)}, u32[]{:S(2)}) collective-permute-start(bf16[8,16384]{1,0:T(8,128)(2,1)S(1)} %get-tuple-element.9), channel_id=1, source_target_pairs={{0,64},{64,0},{1,65},{65,1},{2,66},{66,2},{3,67},{67,3},{4,68},{68... | collective-permute-start | bytes 786440 | tf_op jit(solution)/shard_map/ppermute | solution.py:344
  4.4 0.7 copy-start

commit v5 on v4

--- a/solution.py
+++ b/solution.py
@@ -17,9 +17,8 @@
 EXTRA = 5
 SLOTS = SECT + EXTRA
 SIDE = 4
-OUT_SLOTS = OWNED + 2 * SIDE
-MAIN = 8
-HALF, PLACE = 32, 33
+OUT_SLOTS = OWNED + 2 * SIDE - 1
+MAIN, HELD, LEFT, HALF, PLACE = 8, 24, 40, 44, 45
 
 
 def clip_count(first, count, w):
@@ -50,13 +49,19 @@
             main = jnp.where(held > best, g, main)
             best = jnp.maximum(held, best)
         table_ref[MAIN + w] = main
+        table_ref[HELD + w] = best
+    for g in range(IRREPS):
+        block = jnp.minimum(firsts[g] // OWNED, VIRT - 1)
+        alone = (firsts[g] + counts[g] - 1) // OWNED == block
+        leaves = (table_ref[MAIN + block] != g) & (counts[g] > 0) & jnp.logical_not(alone)
+        table_ref[LEFT + g] = jnp.where(leaves, (block + 1) * OWNED - firsts[g], 0)
     copy.wait()
 
 
 def plan(tile_irreps, blocks):
     return pl.pallas_call(
         plan_kernel,
-        out_shape=(jax.ShapeDtypeStruct((32,), jnp.int32), jax.ShapeDtypeStruct(blocks.shape, blocks.dtype)),
+        out_shape=(jax.ShapeDtypeStruct((HALF,), jnp.int32), jax.ShapeDtypeStruct(blocks.shape, blocks.dtype)),
         in_specs=[pl.BlockSpec(memory_space=pltpu.SMEM), pl.BlockSpec(memory_space=pltpu.HBM)],
         out_specs=(pl.BlockSpec(memory_space=pltpu.SMEM), pl.BlockSpec(memory_space=pltpu.VMEM)),
         scratch_shapes=[pltpu.SemaphoreType.DMA],
@@ -69,8 +74,7 @@
 def position(table_ref, w):
     main = table_ref[MAIN + w]
     first, count = table_ref[main], table_ref[IRREPS + main]
-    before = jnp.maximum(first - w * OWNED, 0)
-    return main, first, count, before, clip_count(first, count, w)
+    return main, first, count, jnp.maximum(first - w * OWNED, 0), table_ref[HELD + w]
 
 
 def pack_kernel(table_ref, own_ref, partner_ref, out_ref, tau_ref):
@@ -188,7 +192,7 @@
                 def _(at):
                     send(low + at, part_ref[:, tile_at(low - row + at)])
 
-    def side(slot, edge, is_left):
+    def side(edge, is_left):
         irrep = irreps_ref[w * OWNED + edge]
         first, count = table_ref[irrep], table_ref[IRREPS + irrep]
         block = (first if is_left else first + count - 1) // OWNED
@@ -210,11 +214,16 @@
             part_ref[...] = lax.dot_general(
                 some_ref[...], block_ref[:, tile_at(at, SIDE)], NN, preferred_element_type=jnp.float32
             )
-            for tile in range(SIDE):
-                send(slot + tile, part_ref[:, tile * TILE : (tile + 1) * TILE])
-
-    side(OWNED, 0, True)
-    side(OWNED + SIDE, OWNED - 1, False)
+            low = 0 if is_left else block * OWNED - first - at
+            size = table_ref[LEFT + irrep] if is_left else first + count - block * OWNED
+            slot = OWNED if is_left else OWNED + table_ref[LEFT + irrep]
+
+            @pl.loop(0, size)
+            def _(tile):
+                send(slot + tile, part_ref[:, tile_at(low + tile)])
+
+    side(0, True)
+    side(OWNED - 1, False)
 
 
 def ladder(table, tile_irreps, taken, blocks):
@@ -237,86 +246,62 @@
     )(table, tile_irreps, taken, blocks)
 
 
-def collect_kernel(table_ref, taken_ref, out_ref, mixed_ref, total_ref, sent, mixed_sent):
-    def copy(w, half):
-        return pltpu.make_async_copy(
-            taken_ref.at[half * VIRT + w, :, : OWNED * TILE], out_ref.at[half, :, tile_at(w * OWNED, OWNED)], sent
-        )
-
-    def mixed_copy(w, half):
-        return pltpu.make_async_copy(
-            mixed_ref.at[half * VIRT + w], out_ref.at[half, :, tile_at(w * OWNED, OWNED)], mixed_sent
-        )
-
-    def is_mixed(w):
-        return position(table_ref, w)[4] < OWNED
+def collect_kernel(table_ref, taken_ref, out_ref, mixed_ref, total_ref, sent):
+    def send(source, w):
+        for half in range(2):
+            pltpu.make_async_copy(
+                source.at[half * VIRT + w, :, : OWNED * TILE], out_ref.at[half, :, tile_at(w * OWNED, OWNED)], sent
+            ).start()
+
+    for w in range(VIRT):
+        pl.when(table_ref[HELD + w] == OWNED)(functools.partial(send, taken_ref, w))
+
+    def mix(w):
+        main = table_ref[MAIN + w]
+        for half in range(2):
+            mixed_ref[half * VIRT + w] = taken_ref[half * VIRT + w, :, : OWNED * TILE]
+
+        @pl.loop(0, IRREPS)
+        def _(irrep):
+            first, count = table_ref[irrep], table_ref[IRREPS + irrep]
+            size = clip_count(first, count, w)
+
+            @pl.when((irrep != main) & (size > 0))
+            def _():
+                left_block, right_block = first // OWNED, (first + count - 1) // OWNED
+                on_left = w == left_block
+                low = jnp.where(on_left, left_block + 1, left_block)
+                high = jnp.where(on_left, right_block + 1, right_block)
+                start = OWNED + jnp.where(on_left, 0, table_ref[LEFT + irrep])
+                slots = tile_at(jnp.minimum(start, OUT_SLOTS - SIDE), SIDE)
+                offset = start - jnp.minimum(start, OUT_SLOTS - SIDE)
+
+                def add(v, totals):
+                    return tuple(
+                        totals[half] + taken_ref[half * VIRT + v, :, slots].astype(jnp.float32) for half in range(2)
+                    )
+
+                zeros = jnp.zeros((ROWS, SIDE * TILE), jnp.float32)
+                totals = lax.fori_loop(low, high, add, (zeros, zeros))
+                for half in range(2):
+                    total_ref[half] = totals[half]
+                tile = jnp.maximum(first - w * OWNED, 0)
+
+                @pl.loop(0, size)
+                def _(at):
+                    columns = tile_at(tile + at)
+                    for half in range(2):
+                        own = taken_ref[half * VIRT + w, :, columns].astype(jnp.float32)
+                        total = own + total_ref[half, :, tile_at(offset + at)]
+                        mixed_ref[half * VIRT + w, :, columns] = total.astype(jnp.bfloat16)
+
+        send(mixed_ref, w)
 
     @pl.loop(0, VIRT)
     def _(w):
-        mixed = is_mixed(w)
-
-        @pl.when(jnp.logical_not(mixed))
-        def _():
-            for half in range(2):
-                copy(w, half).start()
-
-    @pl.loop(0, VIRT)
-    def _(w):
-        @pl.when(is_mixed(w))
-        def _():
-            main = table_ref[MAIN + w]
-            for half in range(2):
-                mixed_ref[half * VIRT + w] = taken_ref[half * VIRT + w, :, : OWNED * TILE]
-
-            @pl.loop(0, IRREPS)
-            def _(irrep):
-                first, count = table_ref[irrep], table_ref[IRREPS + irrep]
-                size = clip_count(first, count, w)
-
-                @pl.when((irrep != main) & (size > 0))
-                def _():
-                    left_block, right_block = first // OWNED, (first + count - 1) // OWNED
-                    on_left = w == left_block
-                    low = jnp.where(on_left, left_block + 1, left_block)
-                    high = jnp.where(on_left, right_block + 1, right_block)
-                    tile = jnp.maximum(first - w * OWNED, 0)
-                    offset = jnp.where(on_left, 0, w * OWNED - first - right_start(first, right_block))
-                    slots = tile_at(jnp.where(on_left, OWNED, OWNED + SIDE), SIDE)
-
-                    def add(v, totals):
-                        return tuple(
-                            totals[half] + taken_ref[half * VIRT + v, :, slots].astype(jnp.float32) for half in range(2)
-                        )
-
-                    zeros = jnp.zeros((ROWS, SIDE * TILE), jnp.float32)
-                    totals = lax.fori_loop(low, high, add, (zeros, zeros))
-                    for half in range(2):
-                        total_ref[half] = totals[half]
-
-                    @pl.loop(0, size)
-                    def _(at):
-                        columns = tile_at(tile + at)
-                        for half in range(2):
-                            own = taken_ref[half * VIRT + w, :, columns].astype(jnp.float32)
-                            total = own + total_ref[half, :, tile_at(offset + at)]
-                            mixed_ref[half * VIRT + w, :, columns] = total.astype(jnp.bfloat16)
-
-            for half in range(2):
-                mixed_copy(w, half).start()
-
-    @pl.loop(0, VIRT)
-    def _(w):
-        mixed = is_mixed(w)
-
-        @pl.when(mixed)
-        def _():
-            for half in range(2):
-                mixed_copy(w, half).wait()
-
-        @pl.when(jnp.logical_not(mixed))
-        def _():
-            for half in range(2):
-                copy(w, half).wait()
+        pl.when(table_ref[HELD + w] < OWNED)(lambda: mix(w))
+
+    pltpu.make_async_copy(out_ref, out_ref, sent).wait()
 
 
 def collect(table, taken):
@@ -328,7 +313,6 @@
         scratch_shapes=[
             pltpu.VMEM((2 * VIRT, ROWS, OWNED * TILE), jnp.bfloat16),
             pltpu.VMEM((2, ROWS, SIDE * TILE), jnp.float32),
-            pltpu.SemaphoreType.DMA,
             pltpu.SemaphoreType.DMA,
         ],
         compiler_params=pltpu.CompilerParams(vmem_limit_bytes=16 << 20),

time: 71.9 us -> 71.5 us (level)
  no operation moved by 1% of the time
where the time goes in v5:
time: 71.5 us; the launch traced here: 71.2 us
  blocking collectives  53.1 us (74%)
  Pallas kernels  12.9 us (18%)
  starting transfers between devices  3.36 us (5%)
  local copies, waits for them, and re-layouts  1.73 us (2%)
    all_to_all x1, blocking collectives, on_device(): lax.all_to_all(packed, 'virt', split_axis=0, concat_axis=0, tiled=True)  31.7 us
    all_to_all x1, blocking collectives, on_device(): lax.all_to_all(sums, ('half', 'virt'), split_axis=0, concat_axis=0, tiled...  21.4 us
    pallas_call x1, Pallas kernels, plan(): pl.pallas_call(plan_kernel, out_shape=(jax.ShapeDtypeStruct((HALF,), jnp....  5.72 us
    pallas_call x1, Pallas kernels, ladder(): pl.pallas_call(ladder_kernel, out_shape=jax.ShapeDtypeStruct((2 * VIRT, R...  4.42 us
    ppermute x1, starting transfers between devices, on_device(): partner = lax.ppermute(sent, 'half', [(0, 1), (1, 0)])  3.36 us
    pallas_call x1, Pallas kernels, collect(): pl.pallas_call(collect_kernel, out_shape=jax.ShapeDtypeStruct((2, ROWS, T...  1.8 us
  transfers between devices with their start and end apart: 1, of which 0 were waited for; matrix products, arithmetic and copies ran while one was open for 0% of the time, Pallas kernels for 8%

profile of v5, /device:TPU:0, one launch (start us, length us, event | category | flops | bytes accessed | tf_op | source)
XLA Modules:
  0.0 71.2 jit_solution(4812452981115654889)
XLA Ops:
  0.0 0.0 copy-start.1
  0.0 1.1 %constant_dynamic-slice_fusion = (bf16[8,16384]{1,0:T(8,128)(2,1)S(1)}, bf16[8,16384]{1,0:T(8,128)(2,1)S(1)}) fusion(bf16[16,16384]{1,0:T(8,128)(2,1)} %param.3, s32[]{:T(128)S(6)} %select_n.7, s32[]{:T(128)S(6)} %select_n.6), kind=kLoop, calls=%fused_computation.1 | loop fusion | bytes 1048584 | tf_op jit(solution)/shard_map/dynamic_slice | solution.py:326
  1.1 3.4 %collective-permute-start = (bf16[8,16384]{1,0:T(8,128)(2,1)S(1)}, bf16[8,16384]{1,0:T(8,128)(2,1)S(1)}, u32[]{:S(2)}, u32[]{:S(2)}) collective-permute-start(bf16[8,16384]{1,0:T(8,128)(2,1)S(1)} %get-tuple-element.9), channel_id=1, source_target_pairs={{0,64},{64,0},{1,65},{65,1},{2,66},{66,2},{3,67},{67,3},{4,68},{68... | collective-permute-start | bytes 786440 | tf_op jit(solution)/shard_map/ppermute | solution.py:328
  4.4 0.0 copy-start
  4.4 0.7 copy-done
  5.1 5.7 %plan.1 = (s32[44]{0:T(128)S(1)}, bf16[1024,6144]{1,0:T(8,128)(2,1)S(1)}) custom-call(s32[128]{0:T(128)S(1)} %copy-done, bf16[1024,6144]{1,0:T(8,128)(2,1)} %blocks_ref.1), custom_call_target="tpu_custom_call" | custom-call | bytes 25165824 | tf_op jit(solution)/shard_map/plan/pallas_call | solution.py:62
  10.8 0.1 pad_add_fusion.table_ref
  10.9 0.0 collective-permute-done.partner_ref
  10.9 1.0 %pack.1 = bf16[16,53,8,128]{3,2,1,0:T(8,128)(2,1)S(1)} custom-call(s32[46]{0:T(128)S(1)} %pad_add_fusion.table_ref, bf16[8,16384]{1,0:T(8,128)(2,1)S(1)} %get-tuple-element.10.own_ref, bf16[8,16384]{1,0:T(8,128)(2,1)S(1)} %collective-permute-done.partner_ref), custom_call_target="tpu_custom_call" | custom-call | tf_op jit(solution)/shard_map/pack/pallas_call | solution.py:99
  11.9 31.7 %all_to_all.10.tau_ref = bf16[16,53,8,128]{3,2,1,0:T(8,128)(2,1)S(1)} all-to-all(bf16[16,53,8,128]{3,2,1,0:T(8,128)(2,1)S(1)} %pack.1), channel_id=1, replica_groups=mesh['half'=2,'quarter'=4,'virt'=16] {'virt'}, dimensions={0} | all-to-all | bytes 3473408 | tf_op jit(solution)/shard_map/all_to_all | solution.py:333
  43.6 0.0 copy-done.1
  43.6 4.4 %ladder.1 = bf16[32,8,1920]{2,1,0:T(8,128)(2,1)S(1)} custom-call(s32[46]{0:T(128)S(1)} %pad_add_fusion.table_ref, s32[128]{0:T(128)S(1)} %copy-done.1, bf16[16,53,8,128]{3,2,1,0:T(8,128)(2,1)S(1)} %all_to_all.10.tau_ref, bf16[1024,6144]{1,0:T(8,128)(2,1)S(1)} %get-tuple-element.8.block_ref), custom_call_target="tpu_custom_call" | custom-call | flops 1610612736 | bytes 16777216 | tf_op jit(solution)/shard_map/ladder/pallas_call | solution.py:231
  48.0 21.4 %all_to_all.11.taken_ref = bf16[32,8,1920]{2,1,0:T(8,128)(2,1)S(1)} all-to-all(bf16[32,8,1920]{2,1,0:T(8,128)(2,1)S(1)} %ladder.1), channel_id=1, replica_groups=mesh['half'=2,'quarter'=4,'virt'=16] {'half','virt'}, dimensions={0} | all-to-all | bytes 1966080 | tf_op jit(solution)/shard_map/all_to_all | solution.py:335
  69.4 1.8 %collect.1 = bf16[2,8,16384]{2,1,0:T(8,128)(2,1)} custom-call(s32[46]{0:T(128)S(1)} %pad_add_fusion.table_ref, bf16[32,8,1920]{2,1,0:T(8,128)(2,1)S(1)} %all_to_all.11.taken_ref), custom_call_target="tpu_custom_call" | custom-call | tf_op jit(solution)/shard_map/collect/pallas_call | solution.py:308
Async XLA Ops:
  0.0 43.6 %copy-start.1 = (s32[128]{0:T(128)S(1)}, s32[128]{0:T(128)}, u32[]{:S(2)}) copy-start(s32[128]{0:T(128)} %irreps_ref.3) | copy-start | bytes 1540
  1.1 9.8 %collective-permute-start = (bf16[8,16384]{1,0:T(8,128)(2,1)S(1)}, bf16[8,16384]{1,0:T(8,128)(2,1)S(1)}, u32[]{:S(2)}, u32[]{:S(2)}) collective-permute-start(bf16[8,16384]{1,0:T(8,128)(2,1)S(1)} %get-tuple-element.9), channel_id=1, source_target_pairs={{0,64},{64,0},{1,65},{65,1},{2,66},{66,2},{3,67},{67,3},{4,68},{68... | collective-permute-start | bytes 786440 | tf_op jit(solution)/shard_map/ppermute | solution.py:328
  4.4 0.7 copy-start

commit v6 on v5

--- a/solution.py
+++ b/solution.py
@@ -16,8 +16,8 @@
 ROWS = 8
 EXTRA = 5
 SLOTS = SECT + EXTRA
-SIDE = 4
-OUT_SLOTS = OWNED + 2 * SIDE - 1
+SIDE = 5
+OUT_SLOTS = OWNED + SIDE
 MAIN, HELD, LEFT, HALF, PLACE = 8, 24, 40, 44, 45
 
 
@@ -46,15 +46,31 @@
         best, main = clip_count(firsts[0], counts[0], w), jnp.int32(0)
         for g in range(1, IRREPS):
             held = clip_count(firsts[g], counts[g], w)
-            main = jnp.where(held > best, g, main)
+            main = jnp.where(held >= best, g, main)
             best = jnp.maximum(held, best)
         table_ref[MAIN + w] = main
         table_ref[HELD + w] = best
+
+    def ends(g):
+        left_block = jnp.minimum(firsts[g] // OWNED, VIRT - 1)
+        right_block = jnp.maximum(firsts[g] + counts[g] - 1, 0) // OWNED
+        wide = (counts[g] > 0) & (left_block != right_block)
+        left = jnp.where(wide & (table_ref[MAIN + left_block] != g), (left_block + 1) * OWNED - firsts[g], 0)
+        right = jnp.where(
+            wide & (table_ref[MAIN + right_block] != g), firsts[g] + counts[g] - right_block * OWNED, 0
+        )
+        return right_block, left, right
+
     for g in range(IRREPS):
-        block = jnp.minimum(firsts[g] // OWNED, VIRT - 1)
-        alone = (firsts[g] + counts[g] - 1) // OWNED == block
-        leaves = (table_ref[MAIN + block] != g) & (counts[g] > 0) & jnp.logical_not(alone)
-        table_ref[LEFT + g] = jnp.where(leaves, (block + 1) * OWNED - firsts[g], 0)
+        right_block, left, right = ends(g)
+
+        @pl.when(left + right > SIDE)
+        def _():
+            table_ref[MAIN + right_block] = jnp.int32(g)
+            table_ref[HELD + right_block] = clip_count(firsts[g], counts[g], right_block)
+
+    for g in range(IRREPS):
+        table_ref[LEFT + g] = ends(g)[1]
     copy.wait()
 
 
@@ -216,7 +232,7 @@
             )
             low = 0 if is_left else block * OWNED - first - at
             size = table_ref[LEFT + irrep] if is_left else first + count - block * OWNED
-            slot = OWNED if is_left else OWNED + table_ref[LEFT + irrep]
+            slot = OWNED if is_left else OUT_SLOTS - size
 
             @pl.loop(0, size)
             def _(tile):
@@ -272,13 +288,11 @@
                 on_left = w == left_block
                 low = jnp.where(on_left, left_block + 1, left_block)
                 high = jnp.where(on_left, right_block + 1, right_block)
-                start = OWNED + jnp.where(on_left, 0, table_ref[LEFT + irrep])
-                slots = tile_at(jnp.minimum(start, OUT_SLOTS - SIDE), SIDE)
-                offset = start - jnp.minimum(start, OUT_SLOTS - SIDE)
+                offset = jnp.where(on_left, 0, SIDE - size)
 
                 def add(v, totals):
                     return tuple(
-                        totals[half] + taken_ref[half * VIRT + v, :, slots].astype(jnp.float32) for half in range(2)
+                        totals[half] + taken_ref[half * VIRT + v, :, OWNED * TILE :].astype(jnp.float32) for half in range(2)
                     )
 
                 zeros = jnp.zeros((ROWS, SIDE * TILE), jnp.float32)

time: 71.5 us -> 71.1 us (level)
  no operation moved by 1% of the time
where the time goes in v6:
time: 71.1 us
  blocking collectives  53 us (75%)
  Pallas kernels  12.9 us (18%)
  starting transfers between devices  3.36 us (5%)
  local copies, waits for them, and re-layouts  1.73 us (2%)
    all_to_all x1, blocking collectives, on_device(): lax.all_to_all(packed, 'virt', split_axis=0, concat_axis=0, tiled=True)  31.7 us
    all_to_all x1, blocking collectives, on_device(): lax.all_to_all(sums, ('half', 'virt'), split_axis=0, concat_axis=0, tiled...  21.3 us
    pallas_call x1, Pallas kernels, plan(): pl.pallas_call(plan_kernel, out_shape=(jax.ShapeDtypeStruct((HALF,), jnp....  5.72 us
    pallas_call x1, Pallas kernels, ladder(): pl.pallas_call(ladder_kernel, out_shape=jax.ShapeDtypeStruct((2 * VIRT, R...  4.48 us
    ppermute x1, starting transfers between devices, on_device(): partner = lax.ppermute(sent, 'half', [(0, 1), (1, 0)])  3.36 us
    pallas_call x1, Pallas kernels, collect(): pl.pallas_call(collect_kernel, out_shape=jax.ShapeDtypeStruct((2, ROWS, T...  1.79 us
  transfers between devices with their start and end apart: 1, of which 0 were waited for; matrix products, arithmetic and copies ran while one was open for 0% of the time, Pallas kernels for 8%

profile of v6, /device:TPU:0, one launch (start us, length us, event | category | flops | bytes accessed | tf_op | source)
XLA Modules:
  0.0 71.1 jit_solution(17006724146603031580)
XLA Ops:
  0.0 0.0 copy-start.1
  0.0 1.1 %constant_dynamic-slice_fusion = (bf16[8,16384]{1,0:T(8,128)(2,1)S(1)}, bf16[8,16384]{1,0:T(8,128)(2,1)S(1)}) fusion(bf16[16,16384]{1,0:T(8,128)(2,1)} %param.3, s32[]{:T(128)S(6)} %select_n.7, s32[]{:T(128)S(6)} %select_n.6), kind=kLoop, calls=%fused_computation.1 | loop fusion | bytes 1048584 | tf_op jit(solution)/shard_map/dynamic_slice | solution.py:340
  1.1 3.4 %collective-permute-start = (bf16[8,16384]{1,0:T(8,128)(2,1)S(1)}, bf16[8,16384]{1,0:T(8,128)(2,1)S(1)}, u32[]{:S(2)}, u32[]{:S(2)}) collective-permute-start(bf16[8,16384]{1,0:T(8,128)(2,1)S(1)} %get-tuple-element.9), channel_id=1, source_target_pairs={{0,64},{64,0},{1,65},{65,1},{2,66},{66,2},{3,67},{67,3},{4,68},{68... | collective-permute-start | bytes 786440 | tf_op jit(solution)/shard_map/ppermute | solution.py:342
  4.4 0.0 copy-start
  4.4 0.7 copy-done
  5.1 5.7 %plan.1 = (s32[44]{0:T(128)S(1)}, bf16[1024,6144]{1,0:T(8,128)(2,1)S(1)}) custom-call(s32[128]{0:T(128)S(1)} %copy-done, bf16[1024,6144]{1,0:T(8,128)(2,1)} %blocks_ref.1), custom_call_target="tpu_custom_call" | custom-call | bytes 25165824 | tf_op jit(solution)/shard_map/plan/pallas_call | solution.py:78
  10.8 0.1 pad_add_fusion.table_ref
  10.9 0.0 collective-permute-done.partner_ref
  10.9 1.0 %pack.1 = bf16[16,53,8,128]{3,2,1,0:T(8,128)(2,1)S(1)} custom-call(s32[46]{0:T(128)S(1)} %pad_add_fusion.table_ref, bf16[8,16384]{1,0:T(8,128)(2,1)S(1)} %get-tuple-element.10.own_ref, bf16[8,16384]{1,0:T(8,128)(2,1)S(1)} %collective-permute-done.partner_ref), custom_call_target="tpu_custom_call" | custom-call | tf_op jit(solution)/shard_map/pack/pallas_call | solution.py:115
  11.9 31.7 %all_to_all.10.tau_ref = bf16[16,53,8,128]{3,2,1,0:T(8,128)(2,1)S(1)} all-to-all(bf16[16,53,8,128]{3,2,1,0:T(8,128)(2,1)S(1)} %pack.1), channel_id=1, replica_groups=mesh['half'=2,'quarter'=4,'virt'=16] {'virt'}, dimensions={0} | all-to-all | bytes 3473408 | tf_op jit(solution)/shard_map/all_to_all | solution.py:347
  43.6 0.0 copy-done.1
  43.6 4.5 %ladder.1 = bf16[32,8,1664]{2,1,0:T(8,128)(2,1)S(1)} custom-call(s32[46]{0:T(128)S(1)} %pad_add_fusion.table_ref, s32[128]{0:T(128)S(1)} %copy-done.1, bf16[16,53,8,128]{3,2,1,0:T(8,128)(2,1)S(1)} %all_to_all.10.tau_ref, bf16[1024,6144]{1,0:T(8,128)(2,1)S(1)} %get-tuple-element.8.block_ref), custom_call_target="tpu_custom_call" | custom-call | flops 1610612736 | bytes 16777216 | tf_op jit(solution)/shard_map/ladder/pallas_call | solution.py:247
  48.0 21.3 %all_to_all.11.taken_ref = bf16[32,8,1664]{2,1,0:T(8,128)(2,1)S(1)} all-to-all(bf16[32,8,1664]{2,1,0:T(8,128)(2,1)S(1)} %ladder.1), channel_id=1, replica_groups=mesh['half'=2,'quarter'=4,'virt'=16] {'half','virt'}, dimensions={0} | all-to-all | bytes 1703936 | tf_op jit(solution)/shard_map/all_to_all | solution.py:349
  69.3 1.8 %collect.1 = bf16[2,8,16384]{2,1,0:T(8,128)(2,1)} custom-call(s32[46]{0:T(128)S(1)} %pad_add_fusion.table_ref, bf16[32,8,1664]{2,1,0:T(8,128)(2,1)S(1)} %all_to_all.11.taken_ref), custom_call_target="tpu_custom_call" | custom-call | tf_op jit(solution)/shard_map/collect/pallas_call | solution.py:322
Async XLA Ops:
  0.0 43.6 %copy-start.1 = (s32[128]{0:T(128)S(1)}, s32[128]{0:T(128)}, u32[]{:S(2)}) copy-start(s32[128]{0:T(128)} %irreps_ref.3) | copy-start | bytes 1540
  1.1 9.8 %collective-permute-start = (bf16[8,16384]{1,0:T(8,128)(2,1)S(1)}, bf16[8,16384]{1,0:T(8,128)(2,1)S(1)}, u32[]{:S(2)}, u32[]{:S(2)}) collective-permute-start(bf16[8,16384]{1,0:T(8,128)(2,1)S(1)} %get-tuple-element.9), channel_id=1, source_target_pairs={{0,64},{64,0},{1,65},{65,1},{2,66},{66,2},{3,67},{67,3},{4,68},{68... | collective-permute-start | bytes 786440 | tf_op jit(solution)/shard_map/ppermute | solution.py:342
  4.4 0.7 copy-start

commit v7 on v6

--- a/solution.py
+++ b/solution.py
@@ -124,6 +124,7 @@
 
 
 GROUP = 2
+NARROW = 3
 SHORT = 32
 NT = (((1,), (1,)), ((), ()))
 NN = (((1,), (0,)), ((), ()))
@@ -132,10 +133,6 @@
 def tile_at(index, count=1):
     start = index * TILE if isinstance(index, int) else pl.multiple_of(index * TILE, TILE)
     return pl.ds(start, count * TILE)
-
-
-def right_start(first, last_block):
-    return jnp.minimum(last_block * OWNED - first, SECT - SIDE)
 
 
 def ladder_kernel(table_ref, irreps_ref, tau_ref, block_ref, out_ref, held_ref, some_ref, part_ref):
@@ -186,20 +183,19 @@
             low = jnp.maximum(first - w * OWNED, 0)
             size = clip_count(first, count, w)
 
-            @pl.when((irrep != main) & (size > 0))
-            def _():
+            def piece(width):
                 column = w * OWNED + low - first
-                start = jnp.minimum(column, SECT - SIDE)
-                row = jnp.minimum(low, OWNED - SIDE)
-                some_ref[...] = jnp.zeros_like(some_ref)
+                start = jnp.minimum(column, SECT - width)
+                row = jnp.minimum(low, OWNED - width)
+                some_ref[:, : width * TILE] = jnp.zeros((VIRT * ROWS, width * TILE), jnp.bfloat16)
 
                 @pl.loop(0, size)
                 def _(at):
                     some_ref[:, tile_at(column - start + at)] = tau_of(low + at)
 
-                part_ref[...] = lax.dot_general(
-                    some_ref[:, : SIDE * TILE],
-                    block_ref[tile_at(row, SIDE), tile_at(start, SIDE)],
+                part_ref[:, : width * TILE] = lax.dot_general(
+                    some_ref[:, : width * TILE],
+                    block_ref[tile_at(row, width), tile_at(start, width)],
                     NT,
                     preferred_element_type=jnp.float32,
                 )
@@ -207,36 +203,35 @@
                 @pl.loop(0, size)
                 def _(at):
                     send(low + at, part_ref[:, tile_at(low - row + at)])
+
+            pl.when((irrep != main) & (size > 0) & (size <= NARROW))(lambda: piece(NARROW))
+            pl.when((irrep != main) & (size > NARROW))(lambda: piece(SIDE))
 
     def side(edge, is_left):
         irrep = irreps_ref[w * OWNED + edge]
         first, count = table_ref[irrep], table_ref[IRREPS + irrep]
         block = (first if is_left else first + count - 1) // OWNED
-
-        @pl.when((block != w) & (table_ref[MAIN + block] != irrep))
-        def _():
+        size = table_ref[LEFT + irrep] if is_left else first + count - block * OWNED
+        slot = OWNED if is_left else OUT_SLOTS - size
+        on = (block != w) & (table_ref[MAIN + block] != irrep)
+
+        def partial(width):
             for tile in range(OWNED):
                 inside = irreps_ref[w * OWNED + tile] == irrep
-
-                @pl.when(inside)
-                def _():
-                    some_ref[:, tile * TILE : (tile + 1) * TILE] = tau_of(tile)
-
-                @pl.when(jnp.logical_not(inside))
-                def _():
-                    some_ref[:, tile * TILE : (tile + 1) * TILE] = jnp.zeros((VIRT * ROWS, TILE), jnp.bfloat16)
-
-            at = 0 if is_left else right_start(first, block)
-            part_ref[...] = lax.dot_general(
-                some_ref[...], block_ref[:, tile_at(at, SIDE)], NN, preferred_element_type=jnp.float32
+                values = tau_of(tile)
+                some_ref[:, tile * TILE : (tile + 1) * TILE] = jnp.where(inside, values, jnp.zeros_like(values))
+            column = 0 if is_left else block * OWNED - first
+            start = 0 if is_left else jnp.minimum(column, SECT - width)
+            part_ref[:, : width * TILE] = lax.dot_general(
+                some_ref[...], block_ref[:, tile_at(start, width)], NN, preferred_element_type=jnp.float32
             )
-            low = 0 if is_left else block * OWNED - first - at
-            size = table_ref[LEFT + irrep] if is_left else first + count - block * OWNED
-            slot = OWNED if is_left else OUT_SLOTS - size
 
             @pl.loop(0, size)
             def _(tile):
-                send(slot + tile, part_ref[:, tile_at(low + tile)])
+                send(slot + tile, part_ref[:, tile_at(column - start + tile)])
+
+        pl.when(on & (size <= NARROW))(lambda: partial(NARROW))
+        pl.when(on & (size > NARROW))(lambda: partial(SIDE))
 
     side(0, True)
     side(OWNED - 1, False)

time: 71.1 us -> 69.5 us (0.977)
  blocking collectives: 53 us -> 51.3 us
    all_to_all x1, blocking collectives: 21.3 us -> 19.6 us  [on_device(): lax.all_to_all(sums, ('half', 'virt'), split_axis=0, concat_axis=0, tiled...]
where the time goes in v7:
time: 69.5 us; the launch traced here: 69.3 us
  blocking collectives  51.3 us (74%)
  Pallas kernels  12.8 us (18%)
  starting transfers between devices  3.36 us (5%)
  local copies, waits for them, and re-layouts  1.73 us (2%)
    all_to_all x1, blocking collectives, on_device(): lax.all_to_all(packed, 'virt', split_axis=0, concat_axis=0, tiled=True)  31.7 us
    all_to_all x1, blocking collectives, on_device(): lax.all_to_all(sums, ('half', 'virt'), split_axis=0, concat_axis=0, tiled...  19.6 us
    pallas_call x1, Pallas kernels, plan(): pl.pallas_call(plan_kernel, out_shape=(jax.ShapeDtypeStruct((HALF,), jnp....  5.72 us
    pallas_call x1, Pallas kernels, ladder(): pl.pallas_call(ladder_kernel, out_shape=jax.ShapeDtypeStruct((2 * VIRT, R...  4.42 us
    ppermute x1, starting transfers between devices, on_device(): partner = lax.ppermute(sent, 'half', [(0, 1), (1, 0)])  3.36 us
    pallas_call x1, Pallas kernels, collect(): pl.pallas_call(collect_kernel, out_shape=jax.ShapeDtypeStruct((2, ROWS, T...  1.68 us
  transfers between devices with their start and end apart: 1, of which 0 were waited for; matrix products, arithmetic and copies ran while one was open for 0% of the time, Pallas kernels for 8%

profile of v7, /device:TPU:0, one launch (start us, length us, event | category | flops | bytes accessed | tf_op | source)
XLA Modules:
  0.0 69.3 jit_solution(8649261636778238943)
XLA Ops:
  0.0 0.0 copy-start.1
  0.0 1.1 %constant_dynamic-slice_fusion = (bf16[8,16384]{1,0:T(8,128)(2,1)S(1)}, bf16[8,16384]{1,0:T(8,128)(2,1)S(1)}) fusion(bf16[16,16384]{1,0:T(8,128)(2,1)} %param.3, s32[]{:T(128)S(6)} %select_n.7, s32[]{:T(128)S(6)} %select_n.6), kind=kLoop, calls=%fused_computation.1 | loop fusion | bytes 1048584 | tf_op jit(solution)/shard_map/dynamic_slice | solution.py:335
  1.1 3.4 %collective-permute-start = (bf16[8,16384]{1,0:T(8,128)(2,1)S(1)}, bf16[8,16384]{1,0:T(8,128)(2,1)S(1)}, u32[]{:S(2)}, u32[]{:S(2)}) collective-permute-start(bf16[8,16384]{1,0:T(8,128)(2,1)S(1)} %get-tuple-element.9), channel_id=1, source_target_pairs={{0,64},{64,0},{1,65},{65,1},{2,66},{66,2},{3,67},{67,3},{4,68},{68... | collective-permute-start | bytes 786440 | tf_op jit(solution)/shard_map/ppermute | solution.py:337
  4.4 0.0 copy-start
  4.4 0.7 copy-done
  5.1 5.7 %plan.1 = (s32[44]{0:T(128)S(1)}, bf16[1024,6144]{1,0:T(8,128)(2,1)S(1)}) custom-call(s32[128]{0:T(128)S(1)} %copy-done, bf16[1024,6144]{1,0:T(8,128)(2,1)} %blocks_ref.1), custom_call_target="tpu_custom_call" | custom-call | bytes 25165824 | tf_op jit(solution)/shard_map/plan/pallas_call | solution.py:78
  10.8 0.1 pad_add_fusion.table_ref
  10.9 0.0 collective-permute-done.partner_ref
  10.9 1.0 %pack.1 = bf16[16,53,8,128]{3,2,1,0:T(8,128)(2,1)S(1)} custom-call(s32[46]{0:T(128)S(1)} %pad_add_fusion.table_ref, bf16[8,16384]{1,0:T(8,128)(2,1)S(1)} %get-tuple-element.10.own_ref, bf16[8,16384]{1,0:T(8,128)(2,1)S(1)} %collective-permute-done.partner_ref), custom_call_target="tpu_custom_call" | custom-call | tf_op jit(solution)/shard_map/pack/pallas_call | solution.py:115
  11.9 31.7 %all_to_all.10.tau_ref = bf16[16,53,8,128]{3,2,1,0:T(8,128)(2,1)S(1)} all-to-all(bf16[16,53,8,128]{3,2,1,0:T(8,128)(2,1)S(1)} %pack.1), channel_id=1, replica_groups=mesh['half'=2,'quarter'=4,'virt'=16] {'virt'}, dimensions={0} | all-to-all | bytes 3473408 | tf_op jit(solution)/shard_map/all_to_all | solution.py:342
  43.6 0.0 copy-done.1
  43.6 4.4 %ladder.1 = bf16[32,8,1664]{2,1,0:T(8,128)(2,1)S(1)} custom-call(s32[46]{0:T(128)S(1)} %pad_add_fusion.table_ref, s32[128]{0:T(128)S(1)} %copy-done.1, bf16[16,53,8,128]{3,2,1,0:T(8,128)(2,1)S(1)} %all_to_all.10.tau_ref, bf16[1024,6144]{1,0:T(8,128)(2,1)S(1)} %get-tuple-element.8.block_ref), custom_call_target="tpu_custom_call" | custom-call | flops 1610612736 | bytes 16777216 | tf_op jit(solution)/shard_map/ladder/pallas_call | solution.py:242
  48.0 19.6 %all_to_all.11.taken_ref = bf16[32,8,1664]{2,1,0:T(8,128)(2,1)S(1)} all-to-all(bf16[32,8,1664]{2,1,0:T(8,128)(2,1)S(1)} %ladder.1), channel_id=1, replica_groups=mesh['half'=2,'quarter'=4,'virt'=16] {'half','virt'}, dimensions={0} | all-to-all | bytes 1703936 | tf_op jit(solution)/shard_map/all_to_all | solution.py:344
  67.6 1.7 %collect.1 = bf16[2,8,16384]{2,1,0:T(8,128)(2,1)} custom-call(s32[46]{0:T(128)S(1)} %pad_add_fusion.table_ref, bf16[32,8,1664]{2,1,0:T(8,128)(2,1)S(1)} %all_to_all.11.taken_ref), custom_call_target="tpu_custom_call" | custom-call | tf_op jit(solution)/shard_map/collect/pallas_call | solution.py:317
Async XLA Ops:
  0.0 43.6 %copy-start.1 = (s32[128]{0:T(128)S(1)}, s32[128]{0:T(128)}, u32[]{:S(2)}) copy-start(s32[128]{0:T(128)} %irreps_ref.3) | copy-start | bytes 1540
  1.1 9.8 %collective-permute-start = (bf16[8,16384]{1,0:T(8,128)(2,1)S(1)}, bf16[8,16384]{1,0:T(8,128)(2,1)S(1)}, u32[]{:S(2)}, u32[]{:S(2)}) collective-permute-start(bf16[8,16384]{1,0:T(8,128)(2,1)S(1)} %get-tuple-element.9), channel_id=1, source_target_pairs={{0,64},{64,0},{1,65},{65,1},{2,66},{66,2},{3,67},{67,3},{4,68},{68... | collective-permute-start | bytes 786440 | tf_op jit(solution)/shard_map/ppermute | solution.py:337
  4.4 0.7 copy-start

commit v8 on v7

--- a/solution.py
+++ b/solution.py
@@ -162,15 +162,24 @@
         def _(slot):
             held_ref[:, tile_at(slot)] = jnp.zeros((VIRT * ROWS, TILE), jnp.bfloat16)
 
-        for start in range(0, OWNED, GROUP):
+        def group(start):
             sums = lax.dot_general(
-                block_ref[start * TILE : (start + GROUP) * TILE, : depth * TILE],
+                block_ref[tile_at(start, GROUP), : depth * TILE],
                 held_ref[:, : depth * TILE],
                 NT,
                 preferred_element_type=jnp.float32,
             )
             for tile in range(GROUP):
                 send(start + tile, sums[tile * TILE : (tile + 1) * TILE].T)
+
+        @pl.when(held == OWNED)
+        def _():
+            for start in range(0, OWNED, GROUP):
+                group(start)
+
+        @pl.when(held < OWNED)
+        def _():
+            pl.loop(before // GROUP, (before + held + GROUP - 1) // GROUP)(lambda at: group(at * GROUP))
 
     pl.when(main_count <= SHORT)(lambda: multiply(SHORT))
     pl.when(main_count > SHORT)(lambda: multiply(SECT))

time: 69.5 us -> 70.1 us (level)
  no operation moved by 1% of the time
where the time goes in v8:
time: 70.1 us; the launch traced here: 69.3 us
  blocking collectives  51.4 us (73%)
  Pallas kernels  12.7 us (18%)
  starting transfers between devices  3.36 us (5%)
  local copies, waits for them, and re-layouts  1.73 us (2%)
    all_to_all x1, blocking collectives, on_device(): lax.all_to_all(packed, 'virt', split_axis=0, concat_axis=0, tiled=True)  31.7 us
    all_to_all x1, blocking collectives, on_device(): lax.all_to_all(sums, ('half', 'virt'), split_axis=0, concat_axis=0, tiled...  19.7 us
    pallas_call x1, Pallas kernels, plan(): pl.pallas_call(plan_kernel, out_shape=(jax.ShapeDtypeStruct((HALF,), jnp....  5.72 us
    pallas_call x1, Pallas kernels, ladder(): pl.pallas_call(ladder_kernel, out_shape=jax.ShapeDtypeStruct((2 * VIRT, R...  4.49 us
    ppermute x1, starting transfers between devices, on_device(): partner = lax.ppermute(sent, 'half', [(0, 1), (1, 0)])  3.36 us
    pallas_call x1, Pallas kernels, collect(): pl.pallas_call(collect_kernel, out_shape=jax.ShapeDtypeStruct((2, ROWS, T...  1.55 us
  transfers between devices with their start and end apart: 1, of which 0 were waited for; matrix products, arithmetic and copies ran while one was open for 0% of the time, Pallas kernels for 8%

profile of v8, /device:TPU:0, one launch (start us, length us, event | category | flops | bytes accessed | tf_op | source)
XLA Modules:
  0.0 69.3 jit_solution(3342755448061198635)
XLA Ops:
  0.0 0.0 copy-start.1
  0.0 1.1 %constant_dynamic-slice_fusion = (bf16[8,16384]{1,0:T(8,128)(2,1)S(1)}, bf16[8,16384]{1,0:T(8,128)(2,1)S(1)}) fusion(bf16[16,16384]{1,0:T(8,128)(2,1)} %param.3, s32[]{:T(128)S(6)} %select_n.7, s32[]{:T(128)S(6)} %select_n.6), kind=kLoop, calls=%fused_computation.1 | loop fusion | bytes 1048584 | tf_op jit(solution)/shard_map/dynamic_slice | solution.py:344
  1.1 3.4 %collective-permute-start = (bf16[8,16384]{1,0:T(8,128)(2,1)S(1)}, bf16[8,16384]{1,0:T(8,128)(2,1)S(1)}, u32[]{:S(2)}, u32[]{:S(2)}) collective-permute-start(bf16[8,16384]{1,0:T(8,128)(2,1)S(1)} %get-tuple-element.9), channel_id=1, source_target_pairs={{0,64},{64,0},{1,65},{65,1},{2,66},{66,2},{3,67},{67,3},{4,68},{68... | collective-permute-start | bytes 786440 | tf_op jit(solution)/shard_map/ppermute | solution.py:346
  4.4 0.0 copy-start
  4.4 0.7 copy-done
  5.1 5.7 %plan.1 = (s32[44]{0:T(128)S(1)}, bf16[1024,6144]{1,0:T(8,128)(2,1)S(1)}) custom-call(s32[128]{0:T(128)S(1)} %copy-done, bf16[1024,6144]{1,0:T(8,128)(2,1)} %blocks_ref.1), custom_call_target="tpu_custom_call" | custom-call | bytes 25165824 | tf_op jit(solution)/shard_map/plan/pallas_call | solution.py:78
  10.8 0.1 pad_add_fusion.table_ref
  10.9 0.0 collective-permute-done.partner_ref
  10.9 1.0 %pack.1 = bf16[16,53,8,128]{3,2,1,0:T(8,128)(2,1)S(1)} custom-call(s32[46]{0:T(128)S(1)} %pad_add_fusion.table_ref, bf16[8,16384]{1,0:T(8,128)(2,1)S(1)} %get-tuple-element.10.own_ref, bf16[8,16384]{1,0:T(8,128)(2,1)S(1)} %collective-permute-done.partner_ref), custom_call_target="tpu_custom_call" | custom-call | tf_op jit(solution)/shard_map/pack/pallas_call | solution.py:115
  11.9 31.7 %all_to_all.10.tau_ref = bf16[16,53,8,128]{3,2,1,0:T(8,128)(2,1)S(1)} all-to-all(bf16[16,53,8,128]{3,2,1,0:T(8,128)(2,1)S(1)} %pack.1), channel_id=1, replica_groups=mesh['half'=2,'quarter'=4,'virt'=16] {'virt'}, dimensions={0} | all-to-all | bytes 3473408 | tf_op jit(solution)/shard_map/all_to_all | solution.py:351
  43.6 0.0 copy-done.1
  43.6 4.5 %ladder.1 = bf16[32,8,1664]{2,1,0:T(8,128)(2,1)S(1)} custom-call(s32[46]{0:T(128)S(1)} %pad_add_fusion.table_ref, s32[128]{0:T(128)S(1)} %copy-done.1, bf16[16,53,8,128]{3,2,1,0:T(8,128)(2,1)S(1)} %all_to_all.10.tau_ref, bf16[1024,6144]{1,0:T(8,128)(2,1)S(1)} %get-tuple-element.8.block_ref), custom_call_target="tpu_custom_call" | custom-call | flops 1610612736 | bytes 16777216 | tf_op jit(solution)/shard_map/ladder/pallas_call | solution.py:251
  48.1 19.7 %all_to_all.11.taken_ref = bf16[32,8,1664]{2,1,0:T(8,128)(2,1)S(1)} all-to-all(bf16[32,8,1664]{2,1,0:T(8,128)(2,1)S(1)} %ladder.1), channel_id=1, replica_groups=mesh['half'=2,'quarter'=4,'virt'=16] {'half','virt'}, dimensions={0} | all-to-all | bytes 1703936 | tf_op jit(solution)/shard_map/all_to_all | solution.py:353
  67.7 1.6 %collect.1 = bf16[2,8,16384]{2,1,0:T(8,128)(2,1)} custom-call(s32[46]{0:T(128)S(1)} %pad_add_fusion.table_ref, bf16[32,8,1664]{2,1,0:T(8,128)(2,1)S(1)} %all_to_all.11.taken_ref), custom_call_target="tpu_custom_call" | custom-call | tf_op jit(solution)/shard_map/collect/pallas_call | solution.py:326
Async XLA Ops:
  0.0 43.6 %copy-start.1 = (s32[128]{0:T(128)S(1)}, s32[128]{0:T(128)}, u32[]{:S(2)}) copy-start(s32[128]{0:T(128)} %irreps_ref.3) | copy-start | bytes 1540
  1.1 9.8 %collective-permute-start = (bf16[8,16384]{1,0:T(8,128)(2,1)S(1)}, bf16[8,16384]{1,0:T(8,128)(2,1)S(1)}, u32[]{:S(2)}, u32[]{:S(2)}) collective-permute-start(bf16[8,16384]{1,0:T(8,128)(2,1)S(1)} %get-tuple-element.9), channel_id=1, source_target_pairs={{0,64},{64,0},{1,65},{65,1},{2,66},{66,2},{3,67},{67,3},{4,68},{68... | collective-permute-start | bytes 786440 | tf_op jit(solution)/shard_map/ppermute | solution.py:346
  4.4 0.7 copy-start
